TPU v7x, 256 devices: a whole 4x4x8 slice. The times are simulated.
256 devices in a mesh: py: 32 (over x_lo, z, core), pz: 8 (over x_hi, y).
Axes of the slice: x: 4 (x_hi: 2, x_lo: 2; x = x_hi * 2 + x_lo), y: 4, z: 8, core: 2. Of those that a mesh axis runs over, the one named last changes fastest.
Arguments:
- velocity: float32 [3, 256, 256, 256], P(None, 'py', 'pz'), may hold values from -6 to 6
- target: float32 [3, 256, 256, 256], P(None, 'py', 'pz'), may hold values from -48 to 48
- closure_weight: float32 [3, 3, 3, 3, 3], replicated, may hold values from -0.625 to 0.625
- closure_bias: float32 [3], replicated, may hold values from -1 to 1
Outputs:
- grad_velocity: float32 [3, 256, 256, 256], P(None, 'py', 'pz')
- grad_weight: float32 [3, 3, 3, 3, 3], replicated
- grad_bias: float32 [3], replicated
- loss: float32 [], replicated
All inputs are finite; a program needn't handle non-finite values.
Results may differ from a plain program's by a relative error of at most 0.0045.
Values may be sent and summed in bfloat16 or wider, within the bound.
A program may use at most 128 MiB of HBM per device.

v0:
```python
import math

import jax
import jax.numpy as jnp
from jax import lax
from jax.sharding import PartitionSpec as P

NX = 256
NY = 256
NZ = 256


time_step = 0.01
viscosity = 0.002


def padded_2(cells, sides, width):
    for axis, dim in sides:
        count = lax.axis_size(axis)
        head = lax.slice_in_dim(cells, 0, width, axis=dim)
        tail = lax.slice_in_dim(cells, cells.shape[dim] - width, cells.shape[dim], axis=dim)
        cells = jnp.concatenate(
            [
                lax.ppermute(tail, axis, [(i, (i + 1) % count) for i in range(count)]),
                cells,
                lax.ppermute(head, axis, [((i + 1) % count, i) for i in range(count)]),
            ],
            axis=dim,
        )
    return cells


def phases(positions, wavenumbers, length):
    turns = positions[:, None] * (wavenumbers[None, :] % length) % length
    angles = turns.astype(jnp.float32) * (2.0 * math.pi / length)
    return (jnp.cos(angles), jnp.sin(angles))


def x_tables(length, kmodes):
    factor = 1.0 / math.sqrt(length)
    cosine, sine_part = phases(jnp.arange(length), jnp.arange(kmodes), length)
    forward = jnp.stack([factor * cosine, -factor * sine_part], axis=1)
    weights = jnp.where(jnp.arange(kmodes) == 0, 1.0, 2.0).astype(jnp.float32)[:, None]
    backward = jnp.stack([weights * factor * cosine.T, -weights * factor * sine_part.T], axis=0)
    return (forward.astype(jnp.bfloat16), backward.astype(jnp.bfloat16))


def line_tables(length, kmodes, mode_total):
    factor = 1.0 / math.sqrt(length)
    wavenumbers = jnp.arange(mode_total) - mode_total // 2
    retained = (jnp.abs(wavenumbers) < kmodes).astype(jnp.float32)[None, :]
    cosine, sine_part = phases(jnp.arange(length), wavenumbers, length)
    real_part = factor * cosine * retained
    imag_part = factor * sine_part * retained
    forward = jnp.stack(
        [jnp.stack([real_part, -imag_part], 1), jnp.stack([imag_part, real_part], 1)], 0
    )
    backward = jnp.stack(
        [jnp.stack([real_part.T, imag_part.T], 1), jnp.stack([-imag_part.T, real_part.T], 1)], 0
    )
    return (forward.astype(jnp.bfloat16), backward.astype(jnp.bfloat16))


def cross_product(left_side, right_side):
    return jnp.stack(
        [
            left_side[1] * right_side[2] - left_side[2] * right_side[1],
            left_side[2] * right_side[0] - left_side[0] * right_side[2],
            left_side[0] * right_side[1] - left_side[1] * right_side[0],
        ],
        0,
    )


def rotate(field, wavenumbers):
    turned = cross_product(wavenumbers, field)
    return jnp.concatenate([-turned[:, :, :, 1:2], turned[:, :, :, 0:1]], axis=3)


def project(field, wavenumbers, square):
    fraction = (
        wavenumbers[0] * field[0] + wavenumbers[1] * field[1] + wavenumbers[2] * field[2]
    ) / jnp.maximum(square, 1.0)
    return field - jnp.stack(
        [wavenumbers[0] * fraction, wavenumbers[1] * fraction, wavenumbers[2] * fraction], 0
    )


def apply_kernel(padded, kernel):
    rows_here = padded.shape[1] - 2
    depth_here = padded.shape[2] - 2
    length = padded.shape[3] - 2
    running = jnp.zeros((kernel.shape[0], rows_here, depth_here, length), jnp.float32)
    for shift_y in range(3):
        for shift_z in range(3):
            for shift_x in range(3):
                window = padded[
                    :,
                    shift_y : shift_y + rows_here,
                    shift_z : shift_z + depth_here,
                    shift_x : shift_x + length,
                ]
                factors = kernel[:, :, shift_y, shift_z, shift_x][:, :, None, None, None]
                running = running + jnp.sum(factors * window[None], axis=1)
    return running


def kernel_sums(misfit, padded):
    rows_here = misfit.shape[1]
    depth_here = misfit.shape[2]
    length = misfit.shape[3]
    outer_list = []
    for shift_y in range(3):
        inner_list = []
        for shift_z in range(3):
            window_slab = padded[
                :, shift_y : shift_y + rows_here, shift_z : shift_z + depth_here, :
            ]
            along_x = [
                jnp.sum(
                    misfit[:, None] * window_slab[None, :, :, :, shift_x : shift_x + length],
                    axis=(2, 3, 4),
                )
                for shift_x in range(3)
            ]
            inner_list.append(jnp.stack(along_x, axis=-1))
        outer_list.append(jnp.stack(inner_list, axis=2))
    return jnp.stack(outer_list, axis=2)


def wrap_ends(padded):
    return jnp.concatenate([padded[..., -1:], padded, padded[..., :1]], axis=3)


def rows_out_joint(shards, section):
    return section(lax.all_to_all(shards, "py", split_axis=2, concat_axis=3, tiled=True))


def cols_out_joint(shards, section):
    return section(lax.all_to_all(shards, "pz", split_axis=3, concat_axis=4, tiled=True))


def cols_back_joint(shards, section):
    return section(lax.all_to_all(shards, "pz", split_axis=3, concat_axis=4, tiled=True))


def rows_back_joint(shards, section):
    return section(lax.all_to_all(shards, "py", split_axis=2, concat_axis=3, tiled=True))


def to_spectral(physical, x_table, y_table, z_table, first_move, second_move):
    components, rows_here, depth_here, length = physical.shape
    row_groups = lax.axis_size("py")
    column_groups = lax.axis_size("pz")
    kmodes = x_table.shape[2]
    x_modes = kmodes // row_groups
    mode_total = y_table.shape[3]
    y_modes = mode_total // column_groups
    z_total = z_table.shape[3]
    x_split = x_table.reshape(length, 2, row_groups, x_modes)
    sectioned = jnp.einsum(
        "cyzx,xrbk->crbkyz", physical, x_split, preferred_element_type=jnp.float32
    ).astype(jnp.bfloat16)
    sectioned = sectioned.reshape(components, 2, row_groups, x_modes * rows_here * depth_here)
    y_split = y_table.reshape(2, row_groups, rows_here, 2, column_groups, y_modes)

    def second_section(shards):
        item_count = shards.shape[0]
        columns_in = shards.reshape(item_count, 2, row_groups, x_modes, rows_here, depth_here)
        result = jnp.einsum(
            "crskyz,rsyqbm->cqkbmz", columns_in, y_split, preferred_element_type=jnp.float32
        ).astype(jnp.bfloat16)
        return result.reshape(item_count, 2, x_modes, column_groups, y_modes * depth_here)

    middle = first_move(sectioned, second_section)
    z_split = z_table.reshape(2, column_groups, depth_here, 2, z_total)

    def third_section(shards):
        item_count = shards.shape[0]
        columns_in = shards.reshape(item_count, 2, x_modes, column_groups, y_modes, depth_here)
        return jnp.einsum(
            "crktmz,rtzqn->ckmqn", columns_in, z_split, preferred_element_type=jnp.float32
        ).astype(jnp.bfloat16)

    return second_move(middle, third_section)


def to_physical(spectral, z_table, y_table, x_table, first_move, second_move):
    components = spectral.shape[0]
    x_modes = spectral.shape[1]
    y_modes = spectral.shape[2]
    z_total = spectral.shape[4]
    row_groups = lax.axis_size("py")
    column_groups = lax.axis_size("pz")
    length = x_table.shape[2]
    rows_here = y_table.shape[3] // row_groups
    depth_here = z_table.shape[3] // column_groups
    z_split = z_table.reshape(2, z_total, 2, column_groups, depth_here)
    sectioned = jnp.einsum(
        "ckmrn,rnqtz->cqktmz", spectral, z_split, preferred_element_type=jnp.float32
    ).astype(jnp.bfloat16)
    sectioned = sectioned.reshape(components, 2, x_modes, column_groups, y_modes * depth_here)
    y_split = y_table.reshape(2, column_groups, y_modes, 2, row_groups, rows_here)

    def second_section(shards):
        item_count = shards.shape[0]
        columns_in = shards.reshape(item_count, 2, x_modes, column_groups, y_modes, depth_here)
        result = jnp.einsum(
            "crktmz,rtmqby->cqbkyz", columns_in, y_split, preferred_element_type=jnp.float32
        ).astype(jnp.bfloat16)
        return result.reshape(item_count, 2, row_groups, x_modes * rows_here * depth_here)

    middle = first_move(sectioned, second_section)
    x_split = x_table.reshape(2, row_groups, x_modes, length)

    def third_section(shards):
        item_count = shards.shape[0]
        columns_in = shards.reshape(item_count, 2, row_groups, x_modes, rows_here, depth_here)
        return jnp.einsum(
            "crskyz,rskx->cyzx", columns_in, x_split, preferred_element_type=jnp.float32
        )

    return second_move(middle, third_section)


def on_device(velocity, target, closure_weight, closure_bias):
    length = NX
    kmodes = length // 4
    y_bound = NY // 4
    z_bound = NZ // 4
    y_total = 2 * y_bound
    x_forward, x_backward = x_tables(length, kmodes)
    y_forward, y_backward = line_tables(NY, y_bound, y_total)
    z_forward, z_backward = line_tables(NZ, z_bound, 2 * z_bound)
    x_modes = kmodes // lax.axis_size("py")
    y_modes = y_total // lax.axis_size("pz")
    wavenumbers = (
        (lax.axis_index("py") * x_modes + jnp.arange(x_modes)).astype(jnp.float32)[
            :, None, None, None
        ],
        (lax.axis_index("pz") * y_modes + jnp.arange(y_modes) - y_bound).astype(jnp.float32)[
            None, :, None, None
        ],
        (jnp.arange(2 * z_bound) - z_bound).astype(jnp.float32)[None, None, None, :],
    )
    square = wavenumbers[0] ** 2 + wavenumbers[1] ** 2 + wavenumbers[2] ** 2
    adjoint_x = jnp.transpose(x_backward, (2, 0, 1))
    adjoint_y = jnp.transpose(y_backward, (2, 3, 0, 1))
    adjoint_z = jnp.transpose(z_backward, (2, 3, 0, 1))
    return_z = jnp.transpose(z_forward, (2, 3, 0, 1))
    return_y = jnp.transpose(y_forward, (2, 3, 0, 1))
    return_x = jnp.transpose(x_forward, (1, 2, 0))

    def forward(field, table_x, table_y, table_z):
        return to_spectral(field, table_x, table_y, table_z, rows_out_joint, cols_out_joint)

    def backward(spectral, table_z, table_y, table_x):
        return to_physical(spectral, table_z, table_y, table_x, cols_back_joint, rows_back_joint)

    velocity_hat = forward(velocity.astype(jnp.bfloat16), x_forward, y_forward, z_forward)
    vorticity_hat = rotate(velocity_hat.astype(jnp.float32), wavenumbers).astype(jnp.bfloat16)
    vorticity = backward(vorticity_hat, z_backward, y_backward, x_backward)
    nonlinear = cross_product(velocity, vorticity).astype(jnp.bfloat16)
    nonlinear_hat = forward(nonlinear, x_forward, y_forward, z_forward)
    rate_hat = (
        project(nonlinear_hat.astype(jnp.float32), wavenumbers, square)
        - viscosity * square * velocity_hat.astype(jnp.float32)
    ).astype(jnp.bfloat16)
    rate_field = backward(rate_hat, z_backward, y_backward, x_backward)
    padded_velocity = wrap_ends(
        padded_2(velocity.astype(jnp.bfloat16), (("py", 1), ("pz", 2)), 1).astype(velocity.dtype)
    )
    closure = apply_kernel(padded_velocity, closure_weight) + closure_bias[:, None, None, None]
    misfit = velocity + time_step * rate_field + closure - target
    loss_part = 0.5 * jnp.sum(misfit * misfit)
    weight_part = kernel_sums(misfit, padded_velocity)
    bias_part = jnp.sum(misfit, axis=(1, 2, 3))
    summed = lax.psum((loss_part, weight_part, bias_part), ("py", "pz"))
    cell_count = float(NX * NY * NZ)
    padded_misfit = wrap_ends(padded_2(misfit, (("py", 1), ("pz", 2)), 1))
    flipped = jnp.transpose(jnp.flip(closure_weight, (2, 3, 4)), (1, 0, 2, 3, 4))
    closure_grad = apply_kernel(padded_misfit, flipped)
    rate_grad = forward((time_step * misfit).astype(jnp.bfloat16), adjoint_x, adjoint_y, adjoint_z)
    projected = project(rate_grad.astype(jnp.float32), wavenumbers, square).astype(jnp.bfloat16)
    nonlinear_grad = backward(projected, return_z, return_y, return_x)
    cross_grad = cross_product(vorticity, nonlinear_grad)
    vorticity_field_grad = cross_product(nonlinear_grad, velocity).astype(jnp.bfloat16)
    vorticity_grad = forward(vorticity_field_grad, adjoint_x, adjoint_y, adjoint_z)
    velocity_grad_hat = (
        rotate(vorticity_grad.astype(jnp.float32), wavenumbers)
        - viscosity * square * rate_grad.astype(jnp.float32)
    ).astype(jnp.bfloat16)
    spectral_grad = backward(velocity_grad_hat, return_z, return_y, return_x)
    grad_velocity = misfit + closure_grad + cross_grad + spectral_grad
    return (grad_velocity, summed[1] / cell_count, summed[2] / cell_count, summed[0] / cell_count)


def solution(mesh):
    in_specs = (P(None, "py", "pz", None), P(None, "py", "pz", None), P(), P())
    out_specs = (P(None, "py", "pz", None), P(), P(), P())
    return jax.shard_map(
        on_device, mesh=mesh, in_specs=in_specs, out_specs=out_specs, check_vma=False
    )
```

profile of v0, /device:TPU:1, one launch (start us, length us, event | category | flops | bytes accessed | tf_op | source)
XLA Modules:
  0.0 562.3 jit_solution(10382256060752247261)
XLA Ops:
  4.4 11.1 %all-to-all-start = ((bf16[3,2,32,512]{3,1,0,2:T(2,128)(2,1)}), bf16[3,2,32,512]{3,1,0,2:T(2,128)(2,1)}, u32[]{:S(2)}, u32[]{:S(2)}) async-start(bf16[3,2,32,512]{3,1,0,2:T(2,128)(2,1)} %reshape.1537), calls=%async_computation | async-start | bytes 393216 | tf_op jit(solution)/shard_map/all_to_all | solution.py:136
  19.9 3.2 negate_convert_fusion
  23.1 3.3 fusion.67
  39.1 3.9 collective-permute-start.3
  65.1 2.9 copy.466
  74.4 4.7 fusion.38
  79.2 3.3 fusion.46
  96.5 4.2 all-to-all-start.1
  100.7 3.1 multiply_reduce_fusion.72
  103.8 3.6 all-to-all-done.1
  112.0 3.4 all-to-all-start.2
  118.3 3.8 all-to-all-done.2
  127.9 12.2 %all-to-all-start.3 = ((bf16[3,2,32,512]{3,1,0,2:T(2,128)(2,1)}), bf16[3,2,32,512]{3,1,0,2:T(2,128)(2,1)S(1)}, u32[]{:S(2)}, u32[]{:S(2)}) async-start(bf16[3,2,32,512]{3,1,0,2:T(2,128)(2,1)} %reshape.1541), calls=%async_computation.3 | async-start | bytes 393216 | tf_op jit(solution)/shard_map/all_to_all | solution.py:148
  140.1 3.0 multiply_reduce_fusion.71
  144.7 5.6 all-to-all-done.3
  158.3 5.4 all-to-all-start.4
  166.2 7.9 %all-to-all-done.4 = bf16[3,2,32,512]{3,1,0,2:T(2,128)(2,1)S(1)} async-done(((bf16[3,2,32,512]{3,1,0,2:T(2,128)(2,1)}), bf16[3,2,32,512]{3,1,0,2:T(2,128)(2,1)S(1)}, u32[]{:S(2)}, u32[]{:S(2)}) %all-to-all-start.4) | async-done | bytes 196640 | tf_op jit(solution)/shard_map/all_to_all | solution.py:136
  175.3 3.1 fusion.23
  180.4 3.5 all-to-all-start.5
  186.4 4.3 all-to-all-done.5
  198.8 3.4 all-to-all-start.6
  204.6 4.4 all-to-all-done.6
  215.7 8.3 %all-to-all-start.7 = ((bf16[3,2,32,512]{3,1,0,2:T(2,128)(2,1)}), bf16[3,2,32,512]{3,1,0,2:T(2,128)(2,1)}, u32[]{:S(2)}, u32[]{:S(2)}) async-start(bf16[3,2,32,512]{3,1,0,2:T(2,128)(2,1)} %reshape.1547), calls=%async_computation.7 | async-start | bytes 393216 | tf_op jit(solution)/shard_map/all_to_all | solution.py:148
  224.1 3.2 multiply_reduce_fusion.58
  230.0 4.4 all-to-all-done.7
  236.9 9.0 %fusion.11 = f32[3,8,32,256]{3,2,1,0:T(8,128)S(1)} fusion(f32[3,8,32,256]{3,2,1,0:T(8,128)} %param.5, f32[3,8,32,256]{3,2,1,0:T(8,128)S(1)} %copy-done, bf16[3,2,32,2,8,32]{5,4,3,1,0,2:T(8,128)(2,1)} %reshape.1548, f32[3,8,32,256]{3,2,1,0:T(8,128)} %get-tuple-element.241, f32[3,8,32,256]{3,2,1,0:T(8,128)} %get-tuple-element.255, ...), kind=kOutput, calls=%fused_computation.146 | convolution fusion | flops 56459264 | bytes 23855116 | tf_op jit(solution)/shard_map/crskyz,rskx->cyzx/dot_general | solution.py:219
  248.2 4.3 multiply_reduce_fusion.26
  254.5 5.2 multiply_reduce_fusion.8
  264.9 7.7 %all-to-all-start.8 = ((bf16[3,2,32,512]{3,1,0,2:T(2,128)(2,1)}), bf16[3,2,32,512]{3,1,0,2:T(2,128)(2,1)}, u32[]{:S(2)}, u32[]{:S(2)}) async-start(bf16[3,2,32,512]{3,1,0,2:T(2,128)(2,1)} %reshape.1549), calls=%async_computation.8 | async-start | bytes 393216 | tf_op jit(solution)/shard_map/all_to_all | solution.py:136
  277.2 75.5 %all-reduce = (f32[3,3,3,3,3]{4,3,1,0,2:T(4,128)}, f32[3]{0:T(128)S(1)}, f32[]{:T(128)}) all-reduce(f32[3,3,3,3,3]{4,3,1,0,2:T(4,128)} %pad_maximum_fusion.10, f32[3]{0:T(128)S(1)} %get-tuple-element.25, f32[]{:T(128)S(6)} %mul_shard_map.3), channel_id=1, replica_groups=mesh['py'=32,'pz'=8] {'py','pz'}, use_global_device_ids=true, to_apply=%region_81.82 | all-reduce | flops 247 | bytes 1976 | tf_op jit(solution)/shard_map/psum | solution.py:278
  355.8 5.1 collective-permute-start.7
  371.5 3.5 fusion.192
  399.7 3.4 all-to-all-start.9
  405.4 4.3 all-to-all-done.9
  420.8 4.2 all-to-all-start.10
  427.3 4.5 all-to-all-done.10
  440.6 9.8 %all-to-all-start.11 = ((bf16[3,2,32,512]{3,1,0,2:T(2,128)(2,1)}), bf16[3,2,32,512]{3,1,0,2:T(2,128)(2,1)}, u32[]{:S(2)}, u32[]{:S(2)}) async-start(bf16[3,2,32,512]{3,1,0,2:T(2,128)(2,1)} %reshape.1553), calls=%async_computation.11 | async-start | bytes 393216 | tf_op jit(solution)/shard_map/all_to_all | solution.py:148
  455.2 5.6 all-to-all-done.11
  469.8 6.0 %all-to-all-start.12 = ((bf16[3,2,32,512]{3,1,0,2:T(2,128)(2,1)}), bf16[3,2,32,512]{3,1,0,2:T(2,128)(2,1)}, u32[]{:S(2)}, u32[]{:S(2)}) async-start(bf16[3,2,32,512]{3,1,0,2:T(2,128)(2,1)} %reshape.1555), calls=%async_computation.12 | async-start | bytes 393216 | tf_op jit(solution)/shard_map/all_to_all | solution.py:136
  480.5 5.7 %all-to-all-done.12 = bf16[3,2,32,512]{3,1,0,2:T(2,128)(2,1)} async-done(((bf16[3,2,32,512]{3,1,0,2:T(2,128)(2,1)}), bf16[3,2,32,512]{3,1,0,2:T(2,128)(2,1)}, u32[]{:S(2)}, u32[]{:S(2)}) %all-to-all-start.12) | async-done | bytes 196640 | tf_op jit(solution)/shard_map/all_to_all | solution.py:136
  488.5 3.0 fusion.21
  495.1 4.0 all-to-all-start.13
  500.2 5.6 %all-to-all-done.13 = bf16[3,2,2,8,512]{4,2,0,1,3:T(2,128)(2,1)} async-done(((bf16[3,2,2,8,512]{4,2,0,1,3:T(2,128)(2,1)}), bf16[3,2,2,8,512]{4,2,0,1,3:T(2,128)(2,1)}, u32[]{:S(2)}, u32[]{:S(2)}) %all-to-all-start.13) | async-done | bytes 98336 | tf_op jit(solution)/shard_map/all_to_all | solution.py:140
  514.9 3.4 all-to-all-start.14
  519.5 5.6 all-to-all-done.14
  531.4 8.5 %all-to-all-start.15 = ((bf16[3,2,32,512]{3,1,0,2:T(2,128)(2,1)}), bf16[3,2,32,512]{3,1,0,2:T(2,128)(2,1)}, u32[]{:S(2)}, u32[]{:S(2)}) async-start(bf16[3,2,32,512]{3,1,0,2:T(2,128)(2,1)} %reshape.1559), calls=%async_computation.15 | async-start | bytes 393216 | tf_op jit(solution)/shard_map/all_to_all | solution.py:148
  543.3 7.0 %all-to-all-done.15 = bf16[3,2,32,512]{3,1,0,2:T(2,128)(2,1)} async-done(((bf16[3,2,32,512]{3,1,0,2:T(2,128)(2,1)}), bf16[3,2,32,512]{3,1,0,2:T(2,128)(2,1)}, u32[]{:S(2)}, u32[]{:S(2)}) %all-to-all-start.15) | async-done | bytes 196640 | tf_op jit(solution)/shard_map/all_to_all | solution.py:148
  551.8 9.2 %fusion.12 = f32[3,8,32,256]{3,2,1,0:T(8,128)} fusion(f32[1,8,32,256]{3,2,1,0:T(8,128)} %get-tuple-element.128, f32[1,8,32,256]{3,2,1,0:T(8,128)} %get-tuple-element.129, f32[1,8,32,256]{3,2,1,0:T(8,128)S(1)} %get-tuple-element.127, bf16[3,2,32,2,8,32]{5,4,3,1,0,2:T(8,128)(2,1)S(1)} %reshape.1560, f32[3,8,32,256]{3,2,1,0:T(8,128)S(1)} %fusion.11, ...), kind=kOutput, calls=%fused_computation.147 | convolution fusion | flops 56426496 | bytes 23855104 | tf_op jit(solution)/shard_map/crskyz,rskx->cyzx/dot_general | solution.py:219
  (529 shorter events, 238.3 us)
Async XLA Ops:
  3.1 24.0 %copy-start.48 = (f32[3,3,3,3,3]{4,3,2,1,0:T(4,128)S(1)}, f32[3,3,3,3,3]{4,3,2,1,0:T(4,128)}, u32[]{:S(2)}) copy-start(f32[3,3,3,3,3]{4,3,2,1,0:T(4,128)} %param.6) | copy-start | bytes 2920
  4.4 86.5 %all-to-all-start = ((bf16[3,2,32,512]{3,1,0,2:T(2,128)(2,1)}), bf16[3,2,32,512]{3,1,0,2:T(2,128)(2,1)}, u32[]{:S(2)}, u32[]{:S(2)}) async-start(bf16[3,2,32,512]{3,1,0,2:T(2,128)(2,1)} %reshape.1537), calls=%async_computation | async-start | bytes 393216 | tf_op jit(solution)/shard_map/all_to_all | solution.py:136
  15.5 21.6 %collective-permute-start = (bf16[3,1,32,256]{3,2,1,0:T(8,128)(2,1)S(1)}, bf16[3,1,32,256]{3,2,1,0:T(8,128)(2,1)S(1)}, u32[]{:S(2)}, u32[]{:S(2)}) collective-permute-start(bf16[3,1,32,256]{3,2,1,0:T(8,128)(2,1)S(1)} %get-tuple-element.164), channel_id=1, source_target_pairs={{0,8},{8,16},{16,24},{24,32},{32,40},{40,48},{48,56},{56,64},{64,7... | collective-permute-start | bytes 147464 | tf_op jit(solution)/shard_map/ppermute | solution.py:24
  17.3 19.9 %collective-permute-start.1 = (bf16[3,1,32,256]{3,2,1,0:T(8,128)(2,1)S(1)}, bf16[3,1,32,256]{3,2,1,0:T(8,128)(2,1)S(1)}, u32[]{:S(2)}, u32[]{:S(2)}) collective-permute-start(bf16[3,1,32,256]{3,2,1,0:T(8,128)(2,1)S(1)} %get-tuple-element.165), channel_id=1, source_target_pairs={{8,0},{16,8},{24,16},{32,24},{40,32},{48,40},{56,48},{64,56},{72,6... | collective-permute-start | bytes 147464 | tf_op jit(solution)/shard_map/ppermute | solution.py:26
  35.2 18.2 %copy-start.79 = (f32[3,3,1,1,1]{4,3,2,0,1:T(1,128)S(1)}, f32[3,3,1,1,1]{4,3,2,0,1:T(1,128)}, u32[]{:S(2)}) copy-start(f32[3,3,1,1,1]{4,3,2,0,1:T(1,128)} %get-tuple-element.184) | copy-start | bytes 112
  35.2 18.9 %copy-start.78 = (f32[3,3,1,1,1]{4,3,2,0,1:T(1,128)S(1)}, f32[3,3,1,1,1]{4,3,2,0,1:T(1,128)}, u32[]{:S(2)}) copy-start(f32[3,3,1,1,1]{4,3,2,0,1:T(1,128)} %get-tuple-element.186) | copy-start | bytes 112
  35.2 19.5 %copy-start.77 = (f32[3,3,1,1,1]{4,3,2,0,1:T(1,128)S(1)}, f32[3,3,1,1,1]{4,3,2,0,1:T(1,128)}, u32[]{:S(2)}) copy-start(f32[3,3,1,1,1]{4,3,2,0,1:T(1,128)} %get-tuple-element.187) | copy-start | bytes 112
  35.2 20.2 %copy-start.76 = (f32[3,3,1,1,1]{4,3,2,0,1:T(1,128)S(1)}, f32[3,3,1,1,1]{4,3,2,0,1:T(1,128)}, u32[]{:S(2)}) copy-start(f32[3,3,1,1,1]{4,3,2,0,1:T(1,128)} %get-tuple-element.189) | copy-start | bytes 112
  35.2 20.9 %copy-start.75 = (f32[3,3,1,1,1]{4,3,2,0,1:T(1,128)S(1)}, f32[3,3,1,1,1]{4,3,2,0,1:T(1,128)}, u32[]{:S(2)}) copy-start(f32[3,3,1,1,1]{4,3,2,0,1:T(1,128)} %get-tuple-element.190) | copy-start | bytes 112
  35.2 21.6 %copy-start.74 = (f32[3,3,1,1,1]{4,3,2,0,1:T(1,128)S(1)}, f32[3,3,1,1,1]{4,3,2,0,1:T(1,128)}, u32[]{:S(2)}) copy-start(f32[3,3,1,1,1]{4,3,2,0,1:T(1,128)} %get-tuple-element.192) | copy-start | bytes 112
  35.2 22.3 %copy-start.73 = (f32[3,3,1,1,1]{4,3,2,0,1:T(1,128)S(1)}, f32[3,3,1,1,1]{4,3,2,0,1:T(1,128)}, u32[]{:S(2)}) copy-start(f32[3,3,1,1,1]{4,3,2,0,1:T(1,128)} %get-tuple-element.193) | copy-start | bytes 112
  35.2 22.9 %copy-start.72 = (f32[3,3,1,1,1]{4,3,2,0,1:T(1,128)S(1)}, f32[3,3,1,1,1]{4,3,2,0,1:T(1,128)}, u32[]{:S(2)}) copy-start(f32[3,3,1,1,1]{4,3,2,0,1:T(1,128)} %get-tuple-element.195) | copy-start | bytes 112
  35.2 23.6 %copy-start.70 = (f32[3,3,1,1,1]{4,3,2,0,1:T(1,128)S(1)}, f32[3,3,1,1,1]{4,3,2,0,1:T(1,128)}, u32[]{:S(2)}) copy-start(f32[3,3,1,1,1]{4,3,2,0,1:T(1,128)} %get-tuple-element.196) | copy-start | bytes 112
  35.2 24.3 %copy-start.68 = (f32[3,3,1,1,1]{4,3,2,0,1:T(1,128)S(1)}, f32[3,3,1,1,1]{4,3,2,0,1:T(1,128)}, u32[]{:S(2)}) copy-start(f32[3,3,1,1,1]{4,3,2,0,1:T(1,128)} %get-tuple-element.198) | copy-start | bytes 112
  35.3 25.0 %copy-start.71 = (f32[3,3,1,1,1]{4,3,2,0,1:T(1,128)S(1)}, f32[3,3,1,1,1]{4,3,2,0,1:T(1,128)}, u32[]{:S(2)}) copy-start(f32[3,3,1,1,1]{4,3,2,0,1:T(1,128)} %get-tuple-element.200) | copy-start | bytes 112
  35.3 25.7 %copy-start.69 = (f32[3,3,1,1,1]{4,3,2,0,1:T(1,128)S(1)}, f32[3,3,1,1,1]{4,3,2,0,1:T(1,128)}, u32[]{:S(2)}) copy-start(f32[3,3,1,1,1]{4,3,2,0,1:T(1,128)} %get-tuple-element.202) | copy-start | bytes 112
  35.3 26.3 %copy-start.67 = (f32[3,3,1,1,1]{4,3,2,0,1:T(1,128)S(1)}, f32[3,3,1,1,1]{4,3,2,0,1:T(1,128)}, u32[]{:S(2)}) copy-start(f32[3,3,1,1,1]{4,3,2,0,1:T(1,128)} %get-tuple-element.203) | copy-start | bytes 112
  35.3 27.0 %copy-start.66 = (f32[3,3,1,1,1]{4,3,2,0,1:T(1,128)S(1)}, f32[3,3,1,1,1]{4,3,2,0,1:T(1,128)}, u32[]{:S(2)}) copy-start(f32[3,3,1,1,1]{4,3,2,0,1:T(1,128)} %get-tuple-element.205) | copy-start | bytes 112
  36.0 28.3 %copy-start.54 = (bf16[256,2,64]{0,2,1:T(8,128)(2,1)S(1)}, bf16[256,2,64]{0,2,1:T(8,128)(2,1)}, u32[]{:S(2)}) copy-start(bf16[256,2,64]{0,2,1:T(8,128)(2,1)} %maximum_bitcast_fusion.23) | copy-start | bytes 196612
  37.8 35.3 %collective-permute-start.2 = (bf16[3,10,1,256]{3,2,1,0:T(2,128)(2,1)}, bf16[3,10,1,256]{3,2,1,0:T(2,128)(2,1)}, u32[]{:S(2)}, u32[]{:S(2)}) collective-permute-start(bf16[3,10,1,256]{3,2,1,0:T(2,128)(2,1)} %get-tuple-element.162), channel_id=1, source_target_pairs={{0,1},{1,2},{2,3},{3,4},{4,5},{5,6},{6,7},{7,0},{8,9},{9,10},{10,1... | collective-permute-start | bytes 46088 | tf_op jit(solution)/shard_map/ppermute | solution.py:24
  39.1 34.0 %collective-permute-start.3 = (bf16[3,10,1,256]{3,2,1,0:T(2,128)(2,1)}, bf16[3,10,1,256]{3,2,1,0:T(2,128)(2,1)}, u32[]{:S(2)}, u32[]{:S(2)}) collective-permute-start(bf16[3,10,1,256]{3,2,1,0:T(2,128)(2,1)} %get-tuple-element.163), channel_id=1, source_target_pairs={{1,0},{2,1},{3,2},{4,3},{5,4},{6,5},{7,6},{0,7},{9,8},{10,9},{11,1... | collective-permute-start | bytes 46088 | tf_op jit(solution)/shard_map/ppermute | solution.py:26
  79.2 36.2 %copy-start.1 = (f32[3,8,32,256]{3,2,1,0:T(8,128)}, f32[3,8,32,256]{3,2,1,0:T(8,128)S(1)}, u32[]{:S(2)}) copy-start(f32[3,8,32,256]{3,2,1,0:T(8,128)S(1)} %get-tuple-element.115) | copy-start | bytes 2359300
  96.5 10.9 %all-to-all-start.1 = ((bf16[3,2,2,8,512]{4,2,0,1,3:T(2,128)(2,1)}), bf16[3,2,2,8,512]{4,2,0,1,3:T(2,128)(2,1)S(1)}, u32[]{:S(2)}, u32[]{:S(2)}) async-start(bf16[3,2,2,8,512]{4,2,0,1,3:T(2,128)(2,1)} %copy.339), calls=%async_computation.1 | async-start | bytes 196608 | tf_op jit(solution)/shard_map/all_to_all | solution.py:140
  112.0 10.1 %all-to-all-start.2 = ((bf16[3,2,2,8,512]{4,2,0,1,3:T(2,128)(2,1)}), bf16[3,2,2,8,512]{4,2,0,1,3:T(2,128)(2,1)S(1)}, u32[]{:S(2)}, u32[]{:S(2)}) async-start(bf16[3,2,2,8,512]{4,2,0,1,3:T(2,128)(2,1)} %copy.341), calls=%async_computation.2 | async-start | bytes 196608 | tf_op jit(solution)/shard_map/all_to_all | solution.py:144
  125.5 17.6 %copy-start.96 = (f32[3,3]{1,0:T(4,128)S(1)}, f32[3,3]{1,0:T(4,128)}, u32[]{:S(2)}) copy-start(f32[3,3]{1,0:T(4,128)} %get-tuple-element.57) | copy-start | bytes 112
  125.5 17.6 %copy-start.133 = (f32[3,3]{1,0:T(4,128)S(1)}, f32[3,3]{1,0:T(4,128)}, u32[]{:S(2)}) copy-start(f32[3,3]{1,0:T(4,128)} %get-tuple-element.80) | copy-start | bytes 112
  127.9 22.4 %all-to-all-start.3 = ((bf16[3,2,32,512]{3,1,0,2:T(2,128)(2,1)}), bf16[3,2,32,512]{3,1,0,2:T(2,128)(2,1)S(1)}, u32[]{:S(2)}, u32[]{:S(2)}) async-start(bf16[3,2,32,512]{3,1,0,2:T(2,128)(2,1)} %reshape.1541), calls=%async_computation.3 | async-start | bytes 393216 | tf_op jit(solution)/shard_map/all_to_all | solution.py:148
  158.3 15.7 %all-to-all-start.4 = ((bf16[3,2,32,512]{3,1,0,2:T(2,128)(2,1)}), bf16[3,2,32,512]{3,1,0,2:T(2,128)(2,1)S(1)}, u32[]{:S(2)}, u32[]{:S(2)}) async-start(bf16[3,2,32,512]{3,1,0,2:T(2,128)(2,1)} %reshape.1543), calls=%async_computation.4 | async-start | bytes 393216 | tf_op jit(solution)/shard_map/all_to_all | solution.py:136
  180.4 10.3 %all-to-all-start.5 = ((bf16[3,2,2,8,512]{4,2,0,1,3:T(2,128)(2,1)}), bf16[3,2,2,8,512]{4,2,0,1,3:T(2,128)(2,1)S(1)}, u32[]{:S(2)}, u32[]{:S(2)}) async-start(bf16[3,2,2,8,512]{4,2,0,1,3:T(2,128)(2,1)} %copy.351), calls=%async_computation.5 | async-start | bytes 196608 | tf_op jit(solution)/shard_map/all_to_all | solution.py:140
  198.8 10.1 %all-to-all-start.6 = ((bf16[3,2,2,8,512]{4,2,0,1,3:T(2,128)(2,1)}), bf16[3,2,2,8,512]{4,2,0,1,3:T(2,128)(2,1)S(1)}, u32[]{:S(2)}, u32[]{:S(2)}) async-start(bf16[3,2,2,8,512]{4,2,0,1,3:T(2,128)(2,1)} %copy.353), calls=%async_computation.6 | async-start | bytes 196608 | tf_op jit(solution)/shard_map/all_to_all | solution.py:144
  215.7 18.7 %all-to-all-start.7 = ((bf16[3,2,32,512]{3,1,0,2:T(2,128)(2,1)}), bf16[3,2,32,512]{3,1,0,2:T(2,128)(2,1)}, u32[]{:S(2)}, u32[]{:S(2)}) async-start(bf16[3,2,32,512]{3,1,0,2:T(2,128)(2,1)} %reshape.1547), calls=%async_computation.7 | async-start | bytes 393216 | tf_op jit(solution)/shard_map/all_to_all | solution.py:148
  260.7 13.3 %collective-permute-start.4 = (f32[3,1,32,256]{3,2,1,0:T(8,128)}, f32[3,1,32,256]{3,2,1,0:T(8,128)S(1)}, u32[]{:S(2)}, u32[]{:S(2)}) collective-permute-start(f32[3,1,32,256]{3,2,1,0:T(8,128)} %get-tuple-element.160), channel_id=1, source_target_pairs={{0,8},{8,16},{16,24},{24,32},{32,40},{40,48},{48,56},{56,64},{64,7... | collective-permute-start | bytes 294920 | tf_op jit(solution)/shard_map/ppermute | solution.py:24
  262.8 11.1 %collective-permute-start.5 = (f32[3,1,32,256]{3,2,1,0:T(8,128)}, f32[3,1,32,256]{3,2,1,0:T(8,128)}, u32[]{:S(2)}, u32[]{:S(2)}) collective-permute-start(f32[3,1,32,256]{3,2,1,0:T(8,128)} %get-tuple-element.161), channel_id=1, source_target_pairs={{8,0},{16,8},{24,16},{32,24},{40,32},{48,40},{56,48},{64,56},{72,6... | collective-permute-start | bytes 294920 | tf_op jit(solution)/shard_map/ppermute | solution.py:26
  264.9 127.5 %all-to-all-start.8 = ((bf16[3,2,32,512]{3,1,0,2:T(2,128)(2,1)}), bf16[3,2,32,512]{3,1,0,2:T(2,128)(2,1)}, u32[]{:S(2)}, u32[]{:S(2)}) async-start(bf16[3,2,32,512]{3,1,0,2:T(2,128)(2,1)} %reshape.1549), calls=%async_computation.8 | async-start | bytes 393216 | tf_op jit(solution)/shard_map/all_to_all | solution.py:136
  355.4 11.0 %collective-permute-start.6 = (f32[3,10,1,256]{3,2,1,0:T(1,128)}, f32[3,10,1,256]{3,2,1,0:T(1,128)S(1)}, u32[]{:S(2)}, u32[]{:S(2)}) collective-permute-start(f32[3,10,1,256]{3,2,1,0:T(1,128)} %get-tuple-element.156), channel_id=1, source_target_pairs={{0,1},{1,2},{2,3},{3,4},{4,5},{5,6},{6,7},{7,0},{8,9},{9,10},{10,1... | collective-permute-start | bytes 92168 | tf_op jit(solution)/shard_map/ppermute | solution.py:24
  355.8 10.6 %collective-permute-start.7 = (f32[3,10,1,256]{3,2,1,0:T(1,128)}, f32[3,10,1,256]{3,2,1,0:T(1,128)}, u32[]{:S(2)}, u32[]{:S(2)}) collective-permute-start(f32[3,10,1,256]{3,2,1,0:T(1,128)} %get-tuple-element.157), channel_id=1, source_target_pairs={{1,0},{2,1},{3,2},{4,3},{5,4},{6,5},{7,6},{0,7},{9,8},{10,9},{11,1... | collective-permute-start | bytes 92168 | tf_op jit(solution)/shard_map/ppermute | solution.py:26
  399.7 10.1 %all-to-all-start.9 = ((bf16[3,2,2,8,512]{4,2,0,1,3:T(2,128)(2,1)}), bf16[3,2,2,8,512]{4,2,0,1,3:T(2,128)(2,1)S(1)}, u32[]{:S(2)}, u32[]{:S(2)}) async-start(bf16[3,2,2,8,512]{4,2,0,1,3:T(2,128)(2,1)} %copy.395), calls=%async_computation.9 | async-start | bytes 196608 | tf_op jit(solution)/shard_map/all_to_all | solution.py:140
  420.8 11.0 %all-to-all-start.10 = ((bf16[3,2,2,8,512]{4,2,0,1,3:T(2,128)(2,1)}), bf16[3,2,2,8,512]{4,2,0,1,3:T(2,128)(2,1)}, u32[]{:S(2)}, u32[]{:S(2)}) async-start(bf16[3,2,2,8,512]{4,2,0,1,3:T(2,128)(2,1)} %copy.399), calls=%async_computation.10 | async-start | bytes 196608 | tf_op jit(solution)/shard_map/all_to_all | solution.py:144
  440.6 20.1 %all-to-all-start.11 = ((bf16[3,2,32,512]{3,1,0,2:T(2,128)(2,1)}), bf16[3,2,32,512]{3,1,0,2:T(2,128)(2,1)}, u32[]{:S(2)}, u32[]{:S(2)}) async-start(bf16[3,2,32,512]{3,1,0,2:T(2,128)(2,1)} %reshape.1553), calls=%async_computation.11 | async-start | bytes 393216 | tf_op jit(solution)/shard_map/all_to_all | solution.py:148
  469.8 16.4 %all-to-all-start.12 = ((bf16[3,2,32,512]{3,1,0,2:T(2,128)(2,1)}), bf16[3,2,32,512]{3,1,0,2:T(2,128)(2,1)}, u32[]{:S(2)}, u32[]{:S(2)}) async-start(bf16[3,2,32,512]{3,1,0,2:T(2,128)(2,1)} %reshape.1555), calls=%async_computation.12 | async-start | bytes 393216 | tf_op jit(solution)/shard_map/all_to_all | solution.py:136
  491.5 19.2 %copy-start.64 = (f32[16]{0:T(128)S(1)}, f32[16]{0:T(128)}, u32[]{:S(2)}) copy-start(f32[16]{0:T(128)} %add_convert_fusion.1) | copy-start | bytes 196
  491.5 19.2 %copy-start.65 = (f32[128]{0:T(128)S(1)}, f32[128]{0:T(128)}, u32[]{:S(2)}) copy-start(f32[128]{0:T(128)} %fusion.166) | copy-start | bytes 1540
  491.5 19.2 %copy-start.108 = (f32[2]{0:T(128)S(1)}, f32[2]{0:T(128)}, u32[]{:S(2)}) copy-start(f32[2]{0:T(128)} %add_convert_fusion) | copy-start | bytes 28
  495.1 10.8 %all-to-all-start.13 = ((bf16[3,2,2,8,512]{4,2,0,1,3:T(2,128)(2,1)}), bf16[3,2,2,8,512]{4,2,0,1,3:T(2,128)(2,1)}, u32[]{:S(2)}, u32[]{:S(2)}) async-start(bf16[3,2,2,8,512]{4,2,0,1,3:T(2,128)(2,1)} %copy.414), calls=%async_computation.13 | async-start | bytes 196608 | tf_op jit(solution)/shard_map/all_to_all | solution.py:140
  500.2 18.1 %copy-start.42 = (f32[3,8,32,256]{3,2,1,0:T(8,128)S(1)}, f32[3,8,32,256]{3,2,1,0:T(8,128)}, u32[]{:S(2)}) copy-start(f32[3,8,32,256]{3,2,1,0:T(8,128)} %get-tuple-element.97) | copy-start | bytes 2359300
  500.2 18.1 %copy-start.110 = (f32[3,3,1,1,1]{1,0,4,3,2:T(4,128)S(1)}, f32[3,3,1,1,1]{1,0,4,3,2:T(4,128)}, u32[]{:S(2)}) copy-start(f32[3,3,1,1,1]{1,0,4,3,2:T(4,128)} %copy.361) | copy-start | bytes 112
  514.9 10.1 %all-to-all-start.14 = ((bf16[3,2,2,8,512]{4,2,0,1,3:T(2,128)(2,1)}), bf16[3,2,2,8,512]{4,2,0,1,3:T(2,128)(2,1)S(1)}, u32[]{:S(2)}, u32[]{:S(2)}) async-start(bf16[3,2,2,8,512]{4,2,0,1,3:T(2,128)(2,1)} %copy.417), calls=%async_computation.14 | async-start | bytes 196608 | tf_op jit(solution)/shard_map/all_to_all | solution.py:144
  531.4 18.9 %all-to-all-start.15 = ((bf16[3,2,32,512]{3,1,0,2:T(2,128)(2,1)}), bf16[3,2,32,512]{3,1,0,2:T(2,128)(2,1)}, u32[]{:S(2)}, u32[]{:S(2)}) async-start(bf16[3,2,32,512]{3,1,0,2:T(2,128)(2,1)} %reshape.1559), calls=%async_computation.15 | async-start | bytes 393216 | tf_op jit(solution)/shard_map/all_to_all | solution.py:148
  (112 other events, 908.4 us)
where the time goes:
time: 574 us; the launch traced here: 562 us
  other arithmetic  121 us (21%)
  local copies, waits for them, and re-layouts  121 us (21%)
  starting transfers between devices  113 us (20%)
  blocking collectives  75.5 us (13%)
  waiting for transfers between devices  72.2 us (13%)
  matrix products  54.7 us (10%)
    psum x1, blocking collectives, on_device(): summed = lax.psum((loss_part, weight_part, bias_part), ('py', 'pz'))  75.5 us
    reduce_sum x40, other arithmetic, apply_kernel(): running = running + jnp.sum(factors * window[None], axis=1)  67.4 us
    all_to_all x4, starting transfers between devices, rows_back_joint(): lax.all_to_all(shards, 'py', split_axis=2, concat_axis=3, tiled=True)  38.8 us
    all_to_all x4, starting transfers between devices, rows_out_joint(): lax.all_to_all(shards, 'py', split_axis=2, concat_axis=3, tiled=True)  30.2 us
    all_to_all x4, waiting for transfers between devices, rows_back_joint(): lax.all_to_all(shards, 'py', split_axis=2, concat_axis=3, tiled=True)  22.5 us
    slice x31, local copies, waits for them, and re-layouts, apply_kernel(): factors = kernel[:, :, shift_y, shift_z, shift_x][:, :, None, None, None]  22 us
    dot_general x4, matrix products, third_section(): jnp.einsum('crskyz,rskx->cyzx', columns_in, x_split, preferred_element_ty...  21.4 us
    all_to_all x4, waiting for transfers between devices, cols_back_joint(): lax.all_to_all(shards, 'pz', split_axis=3, concat_axis=4, tiled=True)  18.2 us
  transfers between devices with their start and end apart: 24, of which 14 were waited for; matrix products, arithmetic and copies ran while one was open for 27% of the time, Pallas kernels for 0%

commit v1 on v0

v1 whole, which is shorter than its diff:
```python
import functools
import math

import jax
import jax.numpy as jnp
import ml_dtypes
import numpy as np
from jax import lax
from jax.experimental import pallas as pl
from jax.experimental.pallas import tpu as pltpu
from jax.sharding import PartitionSpec as P

NX = 256
NY = 256
NZ = 256
PY = 32
PZ = 8
ROWS = NY // PY
DEPTH = NZ // PZ
KX = NX // 4
KL = KX // PZ
MODES = 128
LANES = 128
CELLS = float(NX * NY * NZ)
time_step = 0.01
viscosity = 0.002
MESH = pl.DeviceIdType.MESH
f32 = jnp.float32
bf16 = jnp.bfloat16


def ring(offset, length):
    return min(offset, length - offset)


FAR_PY = sorted(
    [(x, z, c) for x in range(2) for z in range(8) for c in range(2) if x + z + c > 0],
    key=lambda o: (-ring(o[1], 8) - o[0], o[1] > 4, o),
)
FAR_PZ = sorted(
    [(x, y) for x in range(2) for y in range(4) if x + y > 0],
    key=lambda o: (-ring(o[1], 4) - 2 * o[0], o),
)


def phases(positions, wavenumbers, length):
    turns = positions[:, None] * (wavenumbers[None, :] % length) % length
    angles = turns.astype(np.float32) * np.float32(2.0 * math.pi / length)
    return np.cos(angles), np.sin(angles)


def tables():
    factor = np.float32(1.0 / math.sqrt(NX))
    cosine, sine = phases(np.arange(NX), np.arange(KX), NX)
    pair = np.stack([factor * cosine, -factor * sine], axis=0)
    plain = pair.transpose(0, 2, 1).reshape(2, PZ, KL, NX).transpose(1, 0, 2, 3)
    plain = plain.reshape(2 * KX, NX)
    weights = np.where(np.arange(KX) == 0, 1.0, 2.0).astype(np.float32)
    weights = np.broadcast_to(weights.reshape(PZ, 1, KL), (PZ, 2, KL)).reshape(2 * KX, 1)
    wavenumbers = np.arange(MODES) - MODES // 2
    retained = (np.abs(wavenumbers) < MODES // 2).astype(np.float32)[None, :]
    cosine, sine = phases(np.arange(NZ), wavenumbers, NZ)
    real = factor * cosine * retained
    imag = -factor * sine * retained
    z_out = np.concatenate([real, imag], axis=1)
    z_back = np.concatenate([real.T, imag.T], axis=1)
    full = np.stack([np.stack([real, imag], 0), np.stack([-imag, real], 0)], 0)
    y_out = full.reshape(2, 2, PY, ROWS, MODES).transpose(1, 4, 2, 0, 3)
    y_out = y_out.reshape(2 * MODES, 2 * NY)
    given = (plain, plain * weights, z_out, z_back, y_out, y_out.T)
    return tuple(np.ascontiguousarray(t).astype(ml_dtypes.bfloat16) for t in given)


def swap_groups(tiles, lane):
    a0, a1, a2, a3 = tiles
    low = lane < 64
    b0 = jnp.where(low, a0, pltpu.roll(a2, 64, 1))
    b2 = jnp.where(low, pltpu.roll(a0, 64, 1), a2)
    b1 = jnp.where(low, a1, pltpu.roll(a3, 64, 1))
    b3 = jnp.where(low, pltpu.roll(a1, 64, 1), a3)
    even = (lane // 32) % 2 == 0
    c0 = jnp.where(even, b0, pltpu.roll(b1, 32, 1))
    c1 = jnp.where(even, pltpu.roll(b0, 96, 1), b1)
    c2 = jnp.where(even, b2, pltpu.roll(b3, 32, 1))
    c3 = jnp.where(even, pltpu.roll(b2, 96, 1), b3)
    return c0, c1, c2, c3


def dot(left, right, over):
    return lax.dot_general(left, right, (over, ((), ())), preferred_element_type=f32)


def kernel(
    vel, target, weight, flipped, bias, x_plain, x_twice, z_out, z_back, y_out, y_back,
    grad, sums,
    pz_send, pz_recv, py_send, py_recv, field_in, z_in, stage, spec_out,
    vort, push, v_pad, m_pad, v_shift, m_shift, closure, halo_out, halo_in,
    w_parts, r_own, r_pz, r_mid, r_py, hat_v, hat_r,
    pz_ss, pz_rs, py_ss, py_rs, halo_ss, halo_rs, red_ss, red_rs,
):
    py = lax.axis_index("py")
    pz = lax.axis_index("pz")

    barrier = pltpu.get_barrier_semaphore()

    def greet(k, _):
        pl.semaphore_signal(
            barrier, inc=1, device_id=(lax.rem(py + k, PY), pz), device_id_type=MESH
        )
        return 0

    lax.fori_loop(1, PY, greet, 0)
    for k in range(1, PZ):
        pl.semaphore_signal(
            barrier, inc=1, device_id=(py, lax.rem(pz + k, PZ)), device_id_type=MESH
        )

    def remote(src, dst, ss, rs, device):
        return pltpu.make_async_remote_copy(
            src_ref=src, dst_ref=dst, send_sem=ss, recv_sem=rs, device_id=device,
            device_id_type=MESH,
        )

    def send_pz(send_of, recv, ss, rs):
        for dx, dy in FAR_PZ:
            to = lax.rem(pz // 4 + dx, 2) * 4 + lax.rem(lax.rem(pz, 4) + dy, 4)
            remote(send_of(to), recv.at[pz], ss, rs, (py, to)).start()
        pltpu.make_async_copy(send_of(pz), recv.at[pz], rs).start()

    def send_py(send_of, recv, ss, rs):
        x, z, core = py // 16, lax.rem(py, 16) // 2, lax.rem(py, 2)
        for dx, dz, dc in FAR_PY:
            to = lax.rem(x + dx, 2) * 16 + lax.rem(z + dz, 8) * 2 + lax.rem(core + dc, 2)
            remote(send_of(to), recv.at[py], ss, rs, (to, pz)).start()
        pltpu.make_async_copy(send_of(py), recv.at[py], rs).start()

    def arrived(ref, sem):
        pltpu.make_async_copy(ref, ref, sem).wait()

    lane16 = lax.broadcasted_iota(jnp.int32, (16, LANES), 1)
    lane64 = lax.broadcasted_iota(jnp.int32, (64, LANES), 1)

    def halo_y_start(pad, n):
        up = lax.rem(py + 1, PY)
        down = lax.rem(py + PY - 1, PY)
        remote(pad.at[:, ROWS], pad.at[:, 0], halo_ss.at[n], halo_rs.at[n], (up, pz)).start()
        remote(
            pad.at[:, 1], pad.at[:, ROWS + 1], halo_ss.at[n + 1], halo_rs.at[n + 1], (down, pz)
        ).start()

    def halo_z_start(pad, n):
        arrived(pad.at[:, 0], halo_rs.at[n])
        arrived(pad.at[:, ROWS + 1], halo_rs.at[n + 1])
        s = n // 4
        halo_out[s, :, 24:, :] = jnp.zeros((2, 8, NX), f32)
        for j in range(3):
            for y in range(ROWS + 2):
                r = j * (ROWS + 2) + y
                halo_out[s, 0, r : r + 1, :] = pad[j, y, DEPTH - 1 : DEPTH, :]
                halo_out[s, 1, r : r + 1, :] = pad[j, y, 0:1, :]
        up = lax.rem(pz + 1, PZ)
        down = lax.rem(pz + PZ - 1, PZ)
        for side, to in ((0, up), (1, down)):
            remote(
                halo_out.at[s, side], halo_in.at[s, side], halo_ss.at[n + 2 + side],
                halo_rs.at[n + 2 + side], (py, to),
            ).start()

    def shifts(pad, out, n):
        s = n // 4
        arrived(halo_in.at[s, 0], halo_rs.at[n + 2])
        arrived(halo_in.at[s, 1], halo_rs.at[n + 3])
        row = lax.broadcasted_iota(jnp.int32, (DEPTH, NX), 0)
        for j in range(3):
            for y in range(ROWS + 2):
                r = j * (ROWS + 2) + y
                here = pad[j, y]
                below = jnp.where(row == 0, halo_in[s, 0, r : r + 1, :], pltpu.roll(here, 1, 0))
                above = jnp.where(
                    row == DEPTH - 1, halo_in[s, 1, r : r + 1, :], pltpu.roll(here, DEPTH - 1, 0)
                )
                for b, cells in enumerate((below, here, above)):
                    out[j * 9 + b * 3, y] = pltpu.roll(cells, 1, 1)
                    out[j * 9 + b * 3 + 1, y] = cells
                    out[j * 9 + b * 3 + 2, y] = pltpu.roll(cells, NX - 1, 1)

    def convolve_row(shifted, factors, y):
        def step(t, sums_here):
            at = t + (t // 9) * 18
            sums_here = list(sums_here)
            for a in range(3):
                cells = shifted[t, y + a]
                for i in range(3):
                    sums_here[i] = sums_here[i] + factors[i * 81 + a * 9 + at] * cells
            return tuple(sums_here)

        zero = jnp.zeros((DEPTH, NX), f32)
        return lax.fori_loop(0, 27, step, (zero, zero, zero))

    def closure_rows(rows):
        for y in rows:
            for i, cells in enumerate(convolve_row(v_shift, weight, y)):
                closure[i, y] = cells + bias[i]

    def grad_rows(rows):
        for y in rows:
            for i, cells in enumerate(convolve_row(m_shift, flipped, y)):
                closure[i, y] = cells

    def fold(cells):
        total = cells[0:8]
        for k in range(8, DEPTH, 8):
            total = total + cells[k : k + 8]
        return total[:, :LANES] + total[:, LANES:]

    def weight_parts(first, last):
        def one(t, _):
            def row(y, parts):
                parts = list(parts)
                for a in range(3):
                    cells = v_shift[t, y + a]
                    for i in range(3):
                        parts[i * 3 + a] = parts[i * 3 + a] + fold(m_pad[i, y + 1] * cells)
                return tuple(parts)

            zero = jnp.zeros((8, LANES), f32)
            parts = lax.fori_loop(0, ROWS, row, (zero,) * 9)
            at = t + (t // 9) * 18
            for i in range(3):
                for a in range(3):
                    w_parts[i * 81 + a * 9 + at] = parts[i * 3 + a]
            return 0

        lax.fori_loop(first, last, one, 0)

    def reduce_start():
        by_lane = jnp.sum(w_parts[...], axis=1)
        r_own[...] = jnp.sum(by_lane.T, axis=0, keepdims=True) * (1.0 / CELLS)
        send_pz(lambda to: r_own, r_pz, red_ss.at[0], red_rs.at[0])

    def reduce_next():
        arrived(r_pz, red_rs.at[0])
        total = r_pz[0]
        for k in range(1, PZ):
            total = total + r_pz[k]
        r_mid[...] = total
        send_py(lambda to: r_mid, r_py, red_ss.at[1], red_rs.at[1])

    def reduce_end():
        arrived(r_py, red_rs.at[1])
        total = r_py[0]
        for k in range(1, PY):
            total = total + r_py[k]
        sums[...] = total

    lane = lax.broadcasted_iota(jnp.int32, (MODES, LANES), 1)
    group = lane // 32
    kx = (pz * KL + py // 4).astype(f32) + jnp.zeros((MODES, LANES), f32)
    ky = (lax.broadcasted_iota(jnp.int32, (MODES, LANES), 0) - MODES // 2).astype(f32)
    kz = (lane % 32 + (py % 4) * 32 - MODES // 2).astype(f32)
    square = kx * kx + ky * ky + kz * kz

    def pick(first, second, third):
        return jnp.where(group == 0, first, jnp.where(group == 1, second, third))

    def next_one(cells):
        return jnp.where(group == 2, pltpu.roll(cells, 64, 1), pltpu.roll(cells, 96, 1))

    def next_two(cells):
        return jnp.where(group == 0, pltpu.roll(cells, 64, 1), pltpu.roll(cells, 32, 1))

    def turned(cells):
        return pick(ky, kz, kx) * next_two(cells) - pick(kz, kx, ky) * next_one(cells)

    def curl(real, imag):
        return -turned(imag), turned(real)

    def project(cells):
        along = pick(kx, ky, kz)
        part = along * cells
        part = part + next_one(part) + next_two(part)
        return cells - along * (part / jnp.maximum(square, 1.0))

    def out_pz(n):
        send_pz(lambda to: pz_send.at[n, to], pz_recv.at[n], pz_ss.at[n], pz_rs.at[n])

    def out_py(n):
        send_py(lambda to: py_send.at[n, to], py_recv.at[n], py_ss.at[n], py_rs.at[n])

    def in_pz(n):
        arrived(pz_recv.at[n], pz_rs.at[n])

    def in_py(n):
        arrived(py_recv.at[n], py_rs.at[n])

    def x_stage(n, table):
        for t in range(6):
            out = dot(table[...], field_in[t * 128 : (t + 1) * 128, :], ((1,), (1,)))
            out = out.astype(bf16)
            for p in range(PZ):
                pz_send[n, p, t] = out[p * 16 : (p + 1) * 16]

    def z_stage(n):
        in_pz(n)
        for t in range(6):
            for h in range(2):
                tiles = [pz_recv[n, 4 * h + g, t].astype(f32) for g in range(4)]
                for m, tile in enumerate(swap_groups(tiles, lane16)):
                    at = (m * 6 + t) * 16
                    z_in[at : at + 16, h * 128 : (h + 1) * 128] = tile.astype(bf16)
        for m in range(4):
            both = dot(z_in[m * 96 : (m + 1) * 96, :], z_out[...], ((1,), (0,)))
            for c in range(3):
                for h in range(2):
                    at = (c * 2 + h) * 16
                    r0 = both[at : at + 8]
                    r1 = both[at + 8 : at + 16]
                    y = h * 4 + m
                    stage[c, 0, pl.ds(y, 8, stride=8), :] = r0[:, :128] - r1[:, 128:]
                    stage[c, 1, pl.ds(y, 8, stride=8), :] = r0[:, 128:] + r1[:, :128]
        blocks = [
            swap_groups(
                [stage[0, q], stage[1, q], stage[2, q], jnp.zeros((64, LANES), f32)], lane64
            )
            for q in range(2)
        ]
        for g in range(4):
            for k in range(KL):
                py_send[n, k * 4 + g] = jnp.concatenate(
                    [blocks[0][g][k * 8 : k * 8 + 8], blocks[1][g][k * 8 : k * 8 + 8]], axis=0
                ).astype(bf16)

    def y_stage(n):
        in_py(n)
        return dot(y_out[...], py_recv[n].reshape(512, LANES), ((1,), (0,)))

    def y_back_stage(n, modes):
        rows = dot(y_back[...], modes, ((1,), (0,))).astype(bf16)
        for d in range(PY):
            py_send[n, d] = rows[d * 16 : (d + 1) * 16]

    def z_back_stage(n):
        in_py(n)
        for k in range(KL):
            tiles = [py_recv[n, k * 4 + g].astype(f32) for g in range(4)]
            for c, tile in enumerate(swap_groups(tiles, lane16)[:3]):
                at = c * 128 + k * 16
                z_in[at : at + 16, 0:128] = tile.astype(bf16)
        for c in range(3):
            both = dot(z_in[c * 128 : (c + 1) * 128, 0:128], z_back[...], ((1,), (0,)))
            for k in range(KL):
                r0 = both[k * 16 : k * 16 + 8]
                r1 = both[k * 16 + 8 : k * 16 + 16]
                for half in range(2):
                    re = slice(half * 128, half * 128 + 128)
                    im = slice(half * 128 + 256, half * 128 + 384)
                    spec_out[c, half, pl.ds(k, 8, stride=16), :] = r0[:, re] + r1[:, im]
                    spec_out[c, half, pl.ds(8 + k, 8, stride=16), :] = r1[:, re] - r0[:, im]
        for c in range(3):
            for h in range(2):
                for half in range(2):
                    tiles = [
                        spec_out[c, half, (h * 4 + m) * 16 : (h * 4 + m + 1) * 16]
                        for m in range(4)
                    ]
                    for g, tile in enumerate(swap_groups(tiles, lane16)):
                        pz_send[n, half * 4 + g, c * 2 + h] = tile.astype(bf16)

    def x_back_stage(n, table, out):
        in_pz(n)
        for t in range(6):
            block = pz_recv[n, :, t].reshape(128, LANES)
            out(t, dot(block, table[...], ((0,), (0,))))

    def keep(ref):
        def store(t, cells):
            ref[t * 128 : (t + 1) * 128, :] = cells

        return store

    def rows_of(c, y):
        at = (c * ROWS + y) * DEPTH
        return slice(at, at + DEPTH)

    def cross(left, right):
        return (
            left[1] * right[2] - left[2] * right[1],
            left[2] * right[0] - left[0] * right[2],
            left[0] * right[1] - left[1] * right[0],
        )

    for c in range(3):
        for y in range(ROWS):
            cells = vel[c, y]
            v_pad[c, y + 1] = cells
            field_in[rows_of(c, y), :] = cells.astype(bf16)
    x_stage(0, x_plain)
    pl.semaphore_wait(barrier, PY - 1 + PZ - 1)
    out_pz(0)
    halo_y_start(v_pad, 0)
    halo_z_start(v_pad, 0)
    z_stage(0)
    out_py(0)
    shifts(v_pad, v_shift, 0)
    modes = y_stage(0).astype(bf16)
    hat_v[...] = modes
    real, imag = curl(modes[:MODES].astype(f32), modes[MODES:].astype(f32))
    y_back_stage(1, jnp.concatenate([real, imag], axis=0).astype(bf16))
    out_py(1)
    closure_rows(range(0, 4))
    z_back_stage(1)
    out_pz(1)

    closure_rows(range(4, ROWS))
    for c in range(3):
        for y in range(ROWS):
            cells = vel[c, y] + closure[c, y] - target[c, y]
            closure[c, y] = cells
            field_in[rows_of(c, y), :] = (time_step * cells).astype(bf16)
    x_stage(2, x_twice)
    x_back_stage(1, x_twice, keep(vort))
    for y in range(ROWS):
        here = [vel[c, y] for c in range(3)]
        there = [vort[rows_of(c, y), :] for c in range(3)]
        for c, cells in enumerate(cross(here, there)):
            field_in[rows_of(c, y), :] = cells.astype(bf16)
    x_stage(3, x_plain)
    out_pz(3)
    out_pz(2)
    z_stage(3)
    out_py(3)
    z_stage(2)
    out_py(2)
    modes = y_stage(3).astype(bf16).astype(f32)
    drag = viscosity * square
    real = project(modes[:MODES]) - drag * hat_v[:MODES].astype(f32)
    imag = project(modes[MODES:]) - drag * hat_v[MODES:].astype(f32)
    rate_hat = jnp.concatenate([real, imag], axis=0).astype(bf16)
    twice = jnp.where(kx == 0.0, 1.0, 2.0) * (time_step * time_step)
    again = y_stage(2)
    real = (again[:MODES] + twice * rate_hat[:MODES].astype(f32)).astype(bf16)
    imag = (again[MODES:] + twice * rate_hat[MODES:].astype(f32)).astype(bf16)
    hat_r[:MODES] = real
    hat_r[MODES:] = imag
    modes = jnp.concatenate([project(real.astype(f32)), project(imag.astype(f32))], axis=0)
    y_back_stage(4, modes.astype(bf16))
    out_py(4)
    y_back_stage(5, rate_hat)
    out_py(5)
    z_back_stage(4)
    out_pz(4)
    z_back_stage(5)
    out_pz(5)

    x_back_stage(4, x_plain, keep(push))
    for y in range(ROWS):
        here = [vel[c, y] for c in range(3)]
        there = [push[rows_of(c, y), :] for c in range(3)]
        for c, cells in enumerate(cross(there, here)):
            field_in[rows_of(c, y), :] = cells.astype(bf16)
    x_stage(6, x_twice)
    out_pz(6)

    parts = [jnp.zeros((8, LANES), f32) for _ in range(4)]

    def misfit(t, rate):
        c = t // 2
        for m in range(4):
            y = (t % 2) * 4 + m
            cells = closure[c, y] + time_step * rate[m * DEPTH : (m + 1) * DEPTH]
            m_pad[c, y + 1] = cells
            parts[c] = parts[c] + fold(cells)
            parts[3] = parts[3] + fold(cells * cells)

    x_back_stage(5, x_twice, misfit)
    halo_y_start(m_pad, 4)
    for c in range(3):
        w_parts[243 + c] = parts[c]
    w_parts[246] = 0.5 * parts[3]
    for k in range(247, 256):
        w_parts[k] = jnp.zeros((8, LANES), f32)
    z_stage(6)
    out_py(6)
    halo_z_start(m_pad, 4)
    weight_parts(0, 27)
    reduce_start()
    modes = y_stage(6).astype(bf16).astype(f32)
    real, imag = curl(modes[:MODES], modes[MODES:])
    real = real - drag * hat_r[:MODES].astype(f32)
    imag = imag - drag * hat_r[MODES:].astype(f32)
    y_back_stage(7, jnp.concatenate([real, imag], axis=0).astype(bf16))
    out_py(7)
    shifts(m_pad, m_shift, 4)
    reduce_next()
    z_back_stage(7)
    out_pz(7)
    grad_rows(range(ROWS))
    for y in range(ROWS):
        here = [vort[rows_of(c, y), :] for c in range(3)]
        there = [push[rows_of(c, y), :] for c in range(3)]
        for c, cells in enumerate(cross(here, there)):
            closure[c, y] = closure[c, y] + m_pad[c, y + 1] + cells
    reduce_end()

    def finish(t, cells):
        for m in range(4):
            y = (t % 2) * 4 + m
            grad[t // 2, y] = closure[t // 2, y] + cells[m * DEPTH : (m + 1) * DEPTH]

    x_back_stage(7, x_plain, finish)

    for n in range(8):
        arrived(pz_send.at[n, 0 : PZ - 1], pz_ss.at[n])
        arrived(py_send.at[n, 0 : PY - 1], py_ss.at[n])
    for n in (0, 4):
        pad = v_pad if n == 0 else m_pad
        arrived(pad.at[:, 0], halo_ss.at[n])
        arrived(pad.at[:, 0], halo_ss.at[n + 1])
        arrived(halo_out.at[n // 4, 0], halo_ss.at[n + 2])
        arrived(halo_out.at[n // 4, 1], halo_ss.at[n + 3])
    arrived(r_pz.at[0 : PZ - 1], red_ss.at[0])
    arrived(r_py.at[0 : PY - 1], red_ss.at[1])


def on_device(velocity, target, closure_weight, closure_bias):
    shape = velocity.shape
    factors = closure_weight.reshape(243)
    flipped = jnp.transpose(jnp.flip(closure_weight, (2, 3, 4)), (1, 0, 2, 3, 4)).reshape(243)
    given = [jnp.asarray(t) for t in tables()]
    in_vmem = pl.BlockSpec(memory_space=pltpu.VMEM)
    in_smem = pl.BlockSpec(memory_space=pltpu.SMEM)
    dma = pltpu.SemaphoreType.DMA
    pad = (3, ROWS + 2, DEPTH, NX)
    grad, sums = pl.pallas_call(
        kernel,
        out_shape=(
            jax.ShapeDtypeStruct(shape, f32),
            jax.ShapeDtypeStruct((1, 256), f32),
        ),
        in_specs=[in_vmem, in_vmem, in_smem, in_smem, in_smem] + [in_vmem] * 6,
        out_specs=(in_vmem, in_vmem),
        scratch_shapes=[
            pltpu.VMEM((8, PZ, 6, 16, LANES), bf16),
            pltpu.VMEM((8, PZ, 6, 16, LANES), bf16),
            pltpu.VMEM((8, PY, 16, LANES), bf16),
            pltpu.VMEM((8, PY, 16, LANES), bf16),
            pltpu.VMEM((768, NX), bf16),
            pltpu.VMEM((384, 256), bf16),
            pltpu.VMEM((3, 2, 64, LANES), f32),
            pltpu.VMEM((3, 2, 128, LANES), f32),
            pltpu.VMEM((768, NX), f32),
            pltpu.VMEM((768, NX), f32),
            pltpu.VMEM(pad, f32),
            pltpu.VMEM(pad, f32),
            pltpu.VMEM((27, ROWS + 2, DEPTH, NX), f32),
            pltpu.VMEM((27, ROWS + 2, DEPTH, NX), f32),
            pltpu.VMEM((3, ROWS, DEPTH, NX), f32),
            pltpu.VMEM((2, 2, 32, NX), f32),
            pltpu.VMEM((2, 2, 32, NX), f32),
            pltpu.VMEM((256, 8, LANES), f32),
            pltpu.VMEM((1, 256), f32),
            pltpu.VMEM((PZ, 1, 256), f32),
            pltpu.VMEM((1, 256), f32),
            pltpu.VMEM((PY, 1, 256), f32),
            pltpu.VMEM((256, LANES), bf16),
            pltpu.VMEM((256, LANES), bf16),
            dma((8,)), dma((8,)), dma((8,)), dma((8,)), dma((8,)), dma((8,)), dma((2,)), dma((2,)),
        ],
        compiler_params=pltpu.CompilerParams(
            collective_id=0, has_side_effects=True, vmem_limit_bytes=56 << 20
        ),
        name="euler",
    )(velocity, target, factors, flipped, closure_bias, *given)
    return (grad, sums[0, :243].reshape(3, 3, 3, 3, 3), sums[0, 243:246], sums[0, 246])


def solution(mesh):
    in_specs = (P(None, "py", "pz", None), P(None, "py", "pz", None), P(), P())
    out_specs = (P(None, "py", "pz", None), P(), P(), P())
    return jax.shard_map(
        on_device, mesh=mesh, in_specs=in_specs, out_specs=out_specs, check_vma=False
    )
```

time: 574 us -> 103 us (0.18); the launches traced: 562 us -> 103 us
  other arithmetic: 121 us -> 0 us
  local copies, waits for them, and re-layouts: 121 us -> 7.25 us
  starting transfers between devices: 113 us -> 0 us
  Pallas kernels: 0 us -> 95 us
  blocking collectives: 75.5 us -> 0 us
  waiting for transfers between devices: 72.2 us -> 0 us
  matrix products: 54.7 us -> 0 us
    all_to_all x16 -> x0, starting transfers between devices: 98.3 us -> none  [the longest x4 38.8 us: rows_back_joint(): lax.all_to_all(shards, 'py', split_axis=2, concat_axis=3, tiled=True)]
    pallas_call x0 -> x1, Pallas kernels: none -> 95 us  [on_device(): pl.pallas_call(kernel, out_shape=(jax.ShapeDtypeStruct(shape, f32), jax.S...]
    reduce_sum x43 -> x0, other arithmetic: 79.5 us -> none  [the longest x40 67.4 us: apply_kernel(): running = running + jnp.sum(factors * window[None], axis=1)]
    psum x1 -> x0, blocking collectives: 75.5 us -> none  [on_device(): summed = lax.psum((loss_part, weight_part, bias_part), ('py', 'pz'))]
    reshape x52 -> x2, local copies, waits for them, and re-layouts: 75.6 us -> 2.33 us  [the longest x1 1.6 us: on_device(): factors = closure_weight.reshape(243)]
    all_to_all x16 -> x0, waiting for transfers between devices: 72.2 us -> none  [the longest x4 22.5 us: rows_back_joint(): lax.all_to_all(shards, 'py', split_axis=2, concat_axis=3, tiled=True)]
    dot_general x24 -> x0, matrix products: 54.7 us -> none  [the longest x4 21.4 us: third_section(): jnp.einsum('crskyz,rskx->cyzx', columns_in, x_split, preferred_element_ty...]
    slice x41 -> x2, local copies, waits for them, and re-layouts: 32 us -> 0.6 us  [the longest x1 0.58 us: on_device(): sums[0, 246]]
  transfers between devices with their start and end apart: 24 -> 0, of which waited for: 14 -> 0; matrix products, arithmetic and copies ran while one was open for 27% -> 0% of each run, Pallas kernels for 0% -> 0%
where the time goes in v1:
time: 103 us
  Pallas kernels  95 us (92%)
  local copies, waits for them, and re-layouts  7.25 us (7%)
    pallas_call x1, Pallas kernels, on_device(): pl.pallas_call(kernel, out_shape=(jax.ShapeDtypeStruct(shape, f32), jax.S...  95 us
    unnamed x5, local copies, waits for them, and re-layouts  2.75 us

profile of v1, /device:TPU:1, one launch (start us, length us, event | category | flops | bytes accessed | tf_op | source)
XLA Modules:
  0.0 103.0 jit_solution(15873005654103602651)
XLA Ops:
  0.6 0.0 copy-start
  0.6 1.6 %reshape.14.weight = f32[243]{0:T(256)} reshape(f32[3,3,3,3,3]{4,3,2,1,0:T(4,128)} %param.12) | data formatting | bytes 1944 | tf_op jit(solution)/shard_map/reshape | solution.py:527
  2.2 0.0 copy-done
  2.2 0.2 rev.4
  2.4 0.7 reshape.15.flipped
  3.2 95.0 %euler.1 = (f32[3,8,32,256]{3,2,1,0:T(8,128)}, f32[1,256]{1,0:T(1,128)}) custom-call(f32[3,8,32,256]{3,2,1,0:T(8,128)} %vel.1, f32[3,8,32,256]{3,2,1,0:T(8,128)} %target.1, f32[243]{0:T(256)} %reshape.14.weight, f32[243]{0:T(256)} %reshape.15.flipped, f32[3]{0:T(128)} %bias.1, bf16[128,256]{1,0:T(8,128)(2,1)} %constant.12.clone.x_plain, ...), custom_call_target="tpu_custom_call" | custom-call | tf_op jit(solution)/shard_map/euler/pallas_call | solution.py:534
  98.2 0.0 copy-start.1
  98.2 0.7 copy-done.1
  98.9 0.8 reshape_squeeze.3
  99.7 0.6 slice_bitcast_fusion
  100.3 0.6 slice.11
  100.9 2.1 %copy.16 = f32[3,8,32,256]{3,2,1,0:T(8,128)} copy(f32[3,8,32,256]{3,2,1,0:T(8,128)} %get-tuple-element.12) | data formatting | bytes 1572864
  (2 shorter events, 0.0 us)
Async XLA Ops:
  0.6 1.6 %copy-start = (f32[3,3,3,3,3]{4,3,2,1,0:T(4,128)S(1)}, f32[3,3,3,3,3]{4,3,2,1,0:T(4,128)}, u32[]{:S(2)}) copy-start(f32[3,3,3,3,3]{4,3,2,1,0:T(4,128)} %param.12) | copy-start | bytes 2920
  98.2 0.7 copy-start.1

commit v2 on v1

--- a/solution.py
+++ b/solution.py
@@ -91,13 +91,17 @@
 
 
 def kernel(
-    vel, target, weight, flipped, bias, x_plain, x_twice, z_out, z_back, y_out, y_back,
-    grad, sums,
-    pz_send, pz_recv, py_send, py_recv, field_in, z_in, stage, spec_out,
-    vort, push, v_pad, m_pad, v_shift, m_shift, closure, halo_out, halo_in,
-    w_parts, r_own, r_pz, r_mid, r_py, hat_v, hat_r,
-    pz_ss, pz_rs, py_ss, py_rs, halo_ss, halo_rs, red_ss, red_rs,
+    vel_in, target_in, weight, bias, *refs,
 ):
+    tables_in, refs = refs[:6], refs[6:]
+    base_out, last_recv, sums = refs[:3]
+    (x_plain, x_twice, z_out, z_back, y_out, y_back, target), refs = refs[3:10], refs[10:]
+    (
+        pz_send, pz_recv, py_send, py_recv, field_in, z_in, stage, spec_out,
+        vort, push, v_pad, m_pad, v_shift, m_shift, closure, halo_out, halo_in,
+        w_parts, r_own, r_pz, r_mid, r_py, hat_v, hat_r,
+        pz_ss, pz_rs, py_ss, py_rs, halo_ss, halo_rs, red_ss, red_rs, in_sem, base_sem,
+    ) = refs
     py = lax.axis_index("py")
     pz = lax.axis_index("pz")
 
@@ -114,6 +118,20 @@
         pl.semaphore_signal(
             barrier, inc=1, device_id=(py, lax.rem(pz + k, PZ)), device_id_type=MESH
         )
+
+    loads = [pltpu.make_async_copy(tables_in[0], x_plain, in_sem.at[0])]
+    for c in range(3):
+        loads.append(
+            pltpu.make_async_copy(
+                vel_in.at[c], v_pad.at[c, pl.ds(1, ROWS)], in_sem.at[1 + c]
+            )
+        )
+    later = ((2, z_out), (4, y_out), (5, y_back), (3, z_back), (1, x_twice))
+    for k, (at, ref) in enumerate(later):
+        loads.append(pltpu.make_async_copy(tables_in[at], ref, in_sem.at[4 + k]))
+    loads.append(pltpu.make_async_copy(target_in, target, in_sem.at[9]))
+    for load in loads:
+        load.start()
 
     def remote(src, dst, ss, rs, device):
         return pltpu.make_async_remote_copy(
@@ -184,27 +202,32 @@
                     out[j * 9 + b * 3 + 1, y] = cells
                     out[j * 9 + b * 3 + 2, y] = pltpu.roll(cells, NX - 1, 1)
 
-    def convolve_row(shifted, factors, y):
+    def convolve_row(shifted, factor, y):
         def step(t, sums_here):
-            at = t + (t // 9) * 18
             sums_here = list(sums_here)
             for a in range(3):
                 cells = shifted[t, y + a]
                 for i in range(3):
-                    sums_here[i] = sums_here[i] + factors[i * 81 + a * 9 + at] * cells
+                    sums_here[i] = sums_here[i] + factor(i, a, t) * cells
             return tuple(sums_here)
 
         zero = jnp.zeros((DEPTH, NX), f32)
         return lax.fori_loop(0, 27, step, (zero, zero, zero))
 
+    def forward_factor(i, a, t):
+        return weight[i, t // 9, a, (t // 3) % 3, t % 3]
+
+    def backward_factor(i, a, t):
+        return weight[t // 9, i, 2 - a, 2 - (t // 3) % 3, 2 - t % 3]
+
     def closure_rows(rows):
         for y in rows:
-            for i, cells in enumerate(convolve_row(v_shift, weight, y)):
+            for i, cells in enumerate(convolve_row(v_shift, forward_factor, y)):
                 closure[i, y] = cells + bias[i]
 
     def grad_rows(rows):
         for y in rows:
-            for i, cells in enumerate(convolve_row(m_shift, flipped, y)):
+            for i, cells in enumerate(convolve_row(m_shift, backward_factor, y)):
                 closure[i, y] = cells
 
     def fold(cells):
@@ -281,8 +304,9 @@
         part = part + next_one(part) + next_two(part)
         return cells - along * (part / jnp.maximum(square, 1.0))
 
-    def out_pz(n):
-        send_pz(lambda to: pz_send.at[n, to], pz_recv.at[n], pz_ss.at[n], pz_rs.at[n])
+    def out_pz(n, recv=None):
+        recv = pz_recv.at[n] if recv is None else recv
+        send_pz(lambda to: pz_send.at[n, to], recv, pz_ss.at[n], pz_rs.at[n])
 
     def out_py(n):
         send_py(lambda to: py_send.at[n, to], py_recv.at[n], py_ss.at[n], py_rs.at[n])
@@ -294,7 +318,10 @@
         arrived(py_recv.at[n], py_rs.at[n])
 
     def x_stage(n, table):
-        for t in range(6):
+        x_tiles(n, table, range(6))
+
+    def x_tiles(n, table, tiles):
+        for t in tiles:
             out = dot(table[...], field_in[t * 128 : (t + 1) * 128, :], ((1,), (1,)))
             out = out.astype(bf16)
             for p in range(PZ):
@@ -389,15 +416,17 @@
             left[0] * right[1] - left[1] * right[0],
         )
 
+    loads[0].wait()
     for c in range(3):
+        loads[1 + c].wait()
         for y in range(ROWS):
-            cells = vel[c, y]
-            v_pad[c, y + 1] = cells
-            field_in[rows_of(c, y), :] = cells.astype(bf16)
-    x_stage(0, x_plain)
+            field_in[rows_of(c, y), :] = v_pad[c, y + 1].astype(bf16)
+        x_tiles(0, x_plain, (2 * c, 2 * c + 1))
     pl.semaphore_wait(barrier, PY - 1 + PZ - 1)
     out_pz(0)
     halo_y_start(v_pad, 0)
+    for load in loads[4:]:
+        load.wait()
     halo_z_start(v_pad, 0)
     z_stage(0)
     out_py(0)
@@ -414,13 +443,13 @@
     closure_rows(range(4, ROWS))
     for c in range(3):
         for y in range(ROWS):
-            cells = vel[c, y] + closure[c, y] - target[c, y]
+            cells = v_pad[c, y + 1] + closure[c, y] - target[c, y]
             closure[c, y] = cells
             field_in[rows_of(c, y), :] = (time_step * cells).astype(bf16)
     x_stage(2, x_twice)
     x_back_stage(1, x_twice, keep(vort))
     for y in range(ROWS):
-        here = [vel[c, y] for c in range(3)]
+        here = [v_pad[c, y + 1] for c in range(3)]
         there = [vort[rows_of(c, y), :] for c in range(3)]
         for c, cells in enumerate(cross(here, there)):
             field_in[rows_of(c, y), :] = cells.astype(bf16)
@@ -454,7 +483,7 @@
 
     x_back_stage(4, x_plain, keep(push))
     for y in range(ROWS):
-        here = [vel[c, y] for c in range(3)]
+        here = [v_pad[c, y + 1] for c in range(3)]
         there = [push[rows_of(c, y), :] for c in range(3)]
         for c, cells in enumerate(cross(there, here)):
             field_in[rows_of(c, y), :] = cells.astype(bf16)
@@ -493,21 +522,17 @@
     shifts(m_pad, m_shift, 4)
     reduce_next()
     z_back_stage(7)
-    out_pz(7)
+    out_pz(7, last_recv)
     grad_rows(range(ROWS))
     for y in range(ROWS):
         here = [vort[rows_of(c, y), :] for c in range(3)]
         there = [push[rows_of(c, y), :] for c in range(3)]
         for c, cells in enumerate(cross(here, there)):
             closure[c, y] = closure[c, y] + m_pad[c, y + 1] + cells
+    base = pltpu.make_async_copy(closure, base_out, base_sem)
+    base.start()
     reduce_end()
-
-    def finish(t, cells):
-        for m in range(4):
-            y = (t % 2) * 4 + m
-            grad[t // 2, y] = closure[t // 2, y] + cells[m * DEPTH : (m + 1) * DEPTH]
-
-    x_back_stage(7, x_plain, finish)
+    arrived(last_recv, pz_rs.at[7])
 
     for n in range(8):
         arrived(pz_send.at[n, 0 : PZ - 1], pz_ss.at[n])
@@ -520,28 +545,52 @@
         arrived(halo_out.at[n // 4, 1], halo_ss.at[n + 3])
     arrived(r_pz.at[0 : PZ - 1], red_ss.at[0])
     arrived(r_py.at[0 : PY - 1], red_ss.at[1])
+    base.wait()
+
+
+def last_kernel(modes, base, table, sums, grad, grad_weight, grad_bias, loss):
+    block = modes[...].reshape(128, LANES)
+    cells = dot(block, table[...], ((0,), (0,)))
+    for m in range(4):
+        grad[0, m] = base[0, m] + cells[m * DEPTH : (m + 1) * DEPTH]
+
+    @pl.when(pl.program_id(0) == 0)
+    def _():
+        def one(t, _):
+            i, j, a = t // 27, (t // 9) % 3, (t // 3) % 3
+            for e in range(3):
+                grad_weight[i, j, a, t % 3, e] = sums[0, t * 3 + e]
+            return 0
+
+        lax.fori_loop(0, 81, one, 0)
+        for i in range(3):
+            grad_bias[i] = sums[0, 243 + i]
+        loss[0] = sums[0, 246]
 
 
 def on_device(velocity, target, closure_weight, closure_bias):
     shape = velocity.shape
-    factors = closure_weight.reshape(243)
-    flipped = jnp.transpose(jnp.flip(closure_weight, (2, 3, 4)), (1, 0, 2, 3, 4)).reshape(243)
     given = [jnp.asarray(t) for t in tables()]
     in_vmem = pl.BlockSpec(memory_space=pltpu.VMEM)
     in_smem = pl.BlockSpec(memory_space=pltpu.SMEM)
     dma = pltpu.SemaphoreType.DMA
     pad = (3, ROWS + 2, DEPTH, NX)
-    grad, sums = pl.pallas_call(
+    in_hbm = pl.BlockSpec(memory_space=pl.ANY)
+    landing = (PZ, 6, 16, LANES)
+    base, modes, sums = pl.pallas_call(
         kernel,
         out_shape=(
             jax.ShapeDtypeStruct(shape, f32),
+            jax.ShapeDtypeStruct(landing, bf16),
             jax.ShapeDtypeStruct((1, 256), f32),
         ),
-        in_specs=[in_vmem, in_vmem, in_smem, in_smem, in_smem] + [in_vmem] * 6,
-        out_specs=(in_vmem, in_vmem),
-        scratch_shapes=[
-            pltpu.VMEM((8, PZ, 6, 16, LANES), bf16),
-            pltpu.VMEM((8, PZ, 6, 16, LANES), bf16),
+        in_specs=[in_hbm, in_hbm, in_smem, in_smem] + [in_hbm] * 6,
+        out_specs=(in_hbm, in_hbm, in_vmem),
+        scratch_shapes=[pltpu.VMEM(t.shape, bf16) for t in given]
+        + [
+            pltpu.VMEM(shape, f32),
+            pltpu.VMEM((8,) + landing, bf16),
+            pltpu.VMEM((8,) + landing, bf16),
             pltpu.VMEM((8, PY, 16, LANES), bf16),
             pltpu.VMEM((8, PY, 16, LANES), bf16),
             pltpu.VMEM((768, NX), bf16),
@@ -565,13 +614,33 @@
             pltpu.VMEM((256, LANES), bf16),
             pltpu.VMEM((256, LANES), bf16),
             dma((8,)), dma((8,)), dma((8,)), dma((8,)), dma((8,)), dma((8,)), dma((2,)), dma((2,)),
+            dma((10,)), dma,
         ],
         compiler_params=pltpu.CompilerParams(
             collective_id=0, has_side_effects=True, vmem_limit_bytes=56 << 20
         ),
         name="euler",
-    )(velocity, target, factors, flipped, closure_bias, *given)
-    return (grad, sums[0, :243].reshape(3, 3, 3, 3, 3), sums[0, 243:246], sums[0, 246])
+    )(velocity, target, closure_weight, closure_bias, *given)
+    half = pl.BlockSpec((1, 4, DEPTH, NX), lambda t: (t // 2, t % 2, 0, 0))
+    grad, grad_weight, grad_bias, loss = pl.pallas_call(
+        last_kernel,
+        grid=(6,),
+        out_shape=(
+            jax.ShapeDtypeStruct(shape, f32),
+            jax.ShapeDtypeStruct(closure_weight.shape, f32),
+            jax.ShapeDtypeStruct((3,), f32),
+            jax.ShapeDtypeStruct((1,), f32),
+        ),
+        in_specs=[
+            pl.BlockSpec((PZ, 1, 16, LANES), lambda t: (0, t, 0, 0)),
+            half,
+            pl.BlockSpec((128, NX), lambda t: (0, 0)),
+            in_smem,
+        ],
+        out_specs=(half, in_smem, in_smem, in_smem),
+        name="last",
+    )(modes, base, given[0], sums)
+    return grad, grad_weight, grad_bias, loss.reshape(())
 
 
 def solution(mesh):

time: 103 us -> 109 us (1.058)
  Pallas kernels: 95 us -> 108 us
  local copies, waits for them, and re-layouts: 7.25 us -> 0 us
    pallas_call x0 -> x1, Pallas kernels: none -> 8.54 us  [on_device(): pl.pallas_call(last_kernel, grid=(6,), out_shape=(jax.ShapeDtypeStruct(sh...]
    pallas_call x1, Pallas kernels: 95 us -> 99.6 us  [on_device(): pl.pallas_call(kernel, out_shape=(jax.ShapeDtypeStruct(shape, f32), jax.S...]
    unnamed x5 -> x0, local copies, waits for them, and re-layouts: 2.75 us -> none
    reshape x2 -> x0, local copies, waits for them, and re-layouts: 2.33 us -> none  [the longest x1 1.6 us: on_device(): factors = closure_weight.reshape(243)]
where the time goes in v2:
time: 109 us
  Pallas kernels  108 us (99%)
    pallas_call x1, Pallas kernels, on_device(): pl.pallas_call(kernel, out_shape=(jax.ShapeDtypeStruct(shape, f32), jax.S...  99.6 us
    pallas_call x1, Pallas kernels, on_device(): pl.pallas_call(last_kernel, grid=(6,), out_shape=(jax.ShapeDtypeStruct(sh...  8.54 us

profile of v2, /device:TPU:1, one launch (start us, length us, event | category | flops | bytes accessed | tf_op | source)
XLA Modules:
  0.0 108.8 jit_solution(6354614500143756988)
XLA Ops:
  0.6 99.6 %euler.1 = (f32[3,8,32,256]{3,2,1,0:T(8,128)}, bf16[8,6,16,128]{3,2,1,0:T(8,128)(2,1)}, f32[1,256]{1,0:T(1,128)}) custom-call(f32[3,8,32,256]{3,2,1,0:T(8,128)} %vel_in.1, f32[3,8,32,256]{3,2,1,0:T(8,128)} %target_in.1, f32[3,3,3,3,3]{4,3,2,1,0:T(4,128)} %weight.1, f32[3]{0:T(128)} %bias.1, bf16[128,256]{1,0:T(8,128)(2,1)} %constant.12.clone.refs_0_.table, ...), custom_call_target="tpu_custom_call" | custom-call | tf_op jit(solution)/shard_map/euler/pallas_call | solution.py:580
  100.2 8.5 %last.1 = (f32[3,8,32,256]{3,2,1,0:T(8,128)}, f32[3,3,3,3,3]{4,3,2,1,0:T(4,128)}, f32[3]{0:T(128)}, f32[1]{0:T(128)}) custom-call(bf16[8,6,16,128]{3,2,1,0:T(8,128)(2,1)} %get-tuple-element.11.modes, f32[3,8,32,256]{3,2,1,0:T(8,128)} %get-tuple-element.12.base, bf16[128,256]{1,0:T(8,128)(2,1)} %constant.12.clone.refs_0_.table, f32[1,256]{1,0:T(1,128)} %get-tuple-element.13.sums), custom_call_target="tpu_custom_call" | custom-call | tf_op jit(solution)/shard_map/last/pallas_call | solution.py:625

commit v3 on v2

--- a/solution.py
+++ b/solution.py
@@ -91,16 +91,16 @@
 
 
 def kernel(
-    vel_in, target_in, weight, bias, *refs,
+    vel_in, target_in, weight_in, bias, *refs,
 ):
     tables_in, refs = refs[:6], refs[6:]
-    base_out, last_recv, sums = refs[:3]
-    (x_plain, x_twice, z_out, z_back, y_out, y_back, target), refs = refs[3:10], refs[10:]
+    grad, grad_weight, grad_bias, loss = refs[:4]
+    (x_plain, x_twice, z_out, z_back, y_out, y_back, target), refs = refs[4:11], refs[11:]
     (
         pz_send, pz_recv, py_send, py_recv, field_in, z_in, stage, spec_out,
         vort, push, v_pad, m_pad, v_shift, m_shift, closure, halo_out, halo_in,
         w_parts, r_own, r_pz, r_mid, r_py, hat_v, hat_r,
-        pz_ss, pz_rs, py_ss, py_rs, halo_ss, halo_rs, red_ss, red_rs, in_sem, base_sem,
+        pz_ss, pz_rs, py_ss, py_rs, halo_ss, halo_rs, red_ss, red_rs, in_sem, weight, flat,
     ) = refs
     py = lax.axis_index("py")
     pz = lax.axis_index("pz")
@@ -130,6 +130,7 @@
     for k, (at, ref) in enumerate(later):
         loads.append(pltpu.make_async_copy(tables_in[at], ref, in_sem.at[4 + k]))
     loads.append(pltpu.make_async_copy(target_in, target, in_sem.at[9]))
+    loads.append(pltpu.make_async_copy(weight_in, weight, in_sem.at[10]))
     for load in loads:
         load.start()
 
@@ -139,11 +140,11 @@
             device_id_type=MESH,
         )
 
-    def send_pz(send_of, recv, ss, rs):
+    def send_pz(send_of, landing, ss, rs):
         for dx, dy in FAR_PZ:
             to = lax.rem(pz // 4 + dx, 2) * 4 + lax.rem(lax.rem(pz, 4) + dy, 4)
-            remote(send_of(to), recv.at[pz], ss, rs, (py, to)).start()
-        pltpu.make_async_copy(send_of(pz), recv.at[pz], rs).start()
+            remote(send_of(to), landing, ss, rs, (py, to)).start()
+        pltpu.make_async_copy(send_of(pz), landing, rs).start()
 
     def send_py(send_of, recv, ss, rs):
         x, z, core = py // 16, lax.rem(py, 16) // 2, lax.rem(py, 2)
@@ -203,22 +204,33 @@
                     out[j * 9 + b * 3 + 2, y] = pltpu.roll(cells, NX - 1, 1)
 
     def convolve_row(shifted, factor, y):
-        def step(t, sums_here):
+        def step(u, sums_here):
             sums_here = list(sums_here)
-            for a in range(3):
-                cells = shifted[t, y + a]
-                for i in range(3):
-                    sums_here[i] = sums_here[i] + factor(i, a, t) * cells
+            for e in range(3):
+                for a in range(3):
+                    cells = shifted[u * 3 + e, y + a]
+                    for i in range(3):
+                        sums_here[i] = sums_here[i] + factor(i, a, u, e) * cells
             return tuple(sums_here)
 
         zero = jnp.zeros((DEPTH, NX), f32)
-        return lax.fori_loop(0, 27, step, (zero, zero, zero))
-
-    def forward_factor(i, a, t):
-        return weight[i, t // 9, a, (t // 3) % 3, t % 3]
-
-    def backward_factor(i, a, t):
-        return weight[t // 9, i, 2 - a, 2 - (t // 3) % 3, 2 - t % 3]
+        return lax.fori_loop(0, 9, step, (zero, zero, zero))
+
+    def flatten_weight():
+        loads[10].wait()
+
+        def one(t, _):
+            for e in range(3):
+                flat[t * 3 + e] = weight[t // 27, (t // 9) % 3, (t // 3) % 3, t % 3, e]
+            return 0
+
+        lax.fori_loop(0, 81, one, 0)
+
+    def forward_factor(i, a, u, e):
+        return flat[i * 81 + a * 9 + e + u * 3 + (u // 3) * 18]
+
+    def backward_factor(i, a, u, e):
+        return flat[i * 27 + (2 - a) * 9 + 8 - e + (u // 3) * 81 - (u % 3) * 3]
 
     def closure_rows(rows):
         for y in rows:
@@ -240,18 +252,21 @@
         def one(t, _):
             def row(y, parts):
                 parts = list(parts)
-                for a in range(3):
-                    cells = v_shift[t, y + a]
-                    for i in range(3):
-                        parts[i * 3 + a] = parts[i * 3 + a] + fold(m_pad[i, y + 1] * cells)
+                for k in range(0, DEPTH, 8):
+                    here = [m_pad[i, y + 1, k : k + 8] for i in range(3)]
+                    for a in range(3):
+                        cells = v_shift[t, y + a, k : k + 8]
+                        for i in range(3):
+                            parts[i * 3 + a] = parts[i * 3 + a] + here[i] * cells
                 return tuple(parts)
 
-            zero = jnp.zeros((8, LANES), f32)
+            zero = jnp.zeros((8, NX), f32)
             parts = lax.fori_loop(0, ROWS, row, (zero,) * 9)
             at = t + (t // 9) * 18
             for i in range(3):
                 for a in range(3):
-                    w_parts[i * 81 + a * 9 + at] = parts[i * 3 + a]
+                    both = parts[i * 3 + a]
+                    w_parts[i * 81 + a * 9 + at] = both[:, :LANES] + both[:, LANES:]
             return 0
 
         lax.fori_loop(first, last, one, 0)
@@ -259,7 +274,7 @@
     def reduce_start():
         by_lane = jnp.sum(w_parts[...], axis=1)
         r_own[...] = jnp.sum(by_lane.T, axis=0, keepdims=True) * (1.0 / CELLS)
-        send_pz(lambda to: r_own, r_pz, red_ss.at[0], red_rs.at[0])
+        send_pz(lambda to: r_own, r_pz.at[pz], red_ss.at[0], red_rs.at[0])
 
     def reduce_next():
         arrived(r_pz, red_rs.at[0])
@@ -274,7 +289,15 @@
         total = r_py[0]
         for k in range(1, PY):
             total = total + r_py[k]
-        sums[...] = total
+        row = jnp.broadcast_to(total, (8, 256))
+        for t in range(81):
+            here = pltpu.roll(row, (256 - 3 * t) % 256, 1)
+            i, j, a, b = t // 27, (t // 9) % 3, (t // 3) % 3, t % 3
+            grad_weight[i, j, a, b : b + 1, :] = here[0:1, 0:3]
+        at = lax.broadcasted_iota(jnp.int32, (1, 256), 1)
+        for i in range(3):
+            grad_bias[i] = jnp.sum(jnp.where(at == 243 + i, total, 0.0))
+        loss[0] = jnp.sum(jnp.where(at == 246, total, 0.0))
 
     lane = lax.broadcasted_iota(jnp.int32, (MODES, LANES), 1)
     group = lane // 32
@@ -304,47 +327,50 @@
         part = part + next_one(part) + next_two(part)
         return cells - along * (part / jnp.maximum(square, 1.0))
 
-    def out_pz(n, recv=None):
-        recv = pz_recv.at[n] if recv is None else recv
-        send_pz(lambda to: pz_send.at[n, to], recv, pz_ss.at[n], pz_rs.at[n])
+    def out_pz(n, c):
+        tiles = pl.ds(2 * c, 2)
+        send_pz(
+            lambda to: pz_send.at[n, to, tiles], pz_recv.at[n, pz, tiles], pz_ss.at[n],
+            pz_rs.at[n, c],
+        )
 
     def out_py(n):
         send_py(lambda to: py_send.at[n, to], py_recv.at[n], py_ss.at[n], py_rs.at[n])
 
-    def in_pz(n):
-        arrived(pz_recv.at[n], pz_rs.at[n])
+    def in_pz(n, c):
+        here = pz_recv.at[n, :, pl.ds(2 * c, 2)]
+        arrived(here, pz_rs.at[n, c])
 
     def in_py(n):
         arrived(py_recv.at[n], py_rs.at[n])
 
     def x_stage(n, table):
-        x_tiles(n, table, range(6))
-
-    def x_tiles(n, table, tiles):
-        for t in tiles:
+        for c in range(3):
+            x_tiles(n, table, c)
+            out_pz(n, c)
+
+    def x_tiles(n, table, c):
+        for t in (2 * c, 2 * c + 1):
             out = dot(table[...], field_in[t * 128 : (t + 1) * 128, :], ((1,), (1,)))
             out = out.astype(bf16)
             for p in range(PZ):
                 pz_send[n, p, t] = out[p * 16 : (p + 1) * 16]
 
     def z_stage(n):
-        in_pz(n)
-        for t in range(6):
-            for h in range(2):
-                tiles = [pz_recv[n, 4 * h + g, t].astype(f32) for g in range(4)]
-                for m, tile in enumerate(swap_groups(tiles, lane16)):
-                    at = (m * 6 + t) * 16
-                    z_in[at : at + 16, h * 128 : (h + 1) * 128] = tile.astype(bf16)
-        for m in range(4):
-            both = dot(z_in[m * 96 : (m + 1) * 96, :], z_out[...], ((1,), (0,)))
-            for c in range(3):
+        for c in range(3):
+            in_pz(n, c)
+            for yh in range(2):
                 for h in range(2):
-                    at = (c * 2 + h) * 16
-                    r0 = both[at : at + 8]
-                    r1 = both[at + 8 : at + 16]
-                    y = h * 4 + m
-                    stage[c, 0, pl.ds(y, 8, stride=8), :] = r0[:, :128] - r1[:, 128:]
-                    stage[c, 1, pl.ds(y, 8, stride=8), :] = r0[:, 128:] + r1[:, :128]
+                    tiles = [pz_recv[n, 4 * h + g, 2 * c + yh].astype(f32) for g in range(4)]
+                    for m, tile in enumerate(swap_groups(tiles, lane16)):
+                        at = c * 128 + (yh * 4 + m) * 16
+                        z_in[at : at + 16, h * 128 : (h + 1) * 128] = tile.astype(bf16)
+            both = dot(z_in[c * 128 : (c + 1) * 128, :], z_out[...], ((1,), (0,)))
+            for y in range(ROWS):
+                r0 = both[y * 16 : y * 16 + 8]
+                r1 = both[y * 16 + 8 : y * 16 + 16]
+                stage[c, 0, pl.ds(y, 8, stride=8), :] = r0[:, :128] - r1[:, 128:]
+                stage[c, 1, pl.ds(y, 8, stride=8), :] = r0[:, 128:] + r1[:, :128]
         blocks = [
             swap_groups(
                 [stage[0, q], stage[1, q], stage[2, q], jnp.zeros((64, LANES), f32)], lane64
@@ -383,7 +409,6 @@
                     im = slice(half * 128 + 256, half * 128 + 384)
                     spec_out[c, half, pl.ds(k, 8, stride=16), :] = r0[:, re] + r1[:, im]
                     spec_out[c, half, pl.ds(8 + k, 8, stride=16), :] = r1[:, re] - r0[:, im]
-        for c in range(3):
             for h in range(2):
                 for half in range(2):
                     tiles = [
@@ -392,12 +417,14 @@
                     ]
                     for g, tile in enumerate(swap_groups(tiles, lane16)):
                         pz_send[n, half * 4 + g, c * 2 + h] = tile.astype(bf16)
+            out_pz(n, c)
 
     def x_back_stage(n, table, out):
-        in_pz(n)
-        for t in range(6):
-            block = pz_recv[n, :, t].reshape(128, LANES)
-            out(t, dot(block, table[...], ((0,), (0,))))
+        for c in range(3):
+            in_pz(n, c)
+            for t in (2 * c, 2 * c + 1):
+                block = pz_recv[n, :, t].reshape(128, LANES)
+                out(t, dot(block, table[...], ((0,), (0,))))
 
     def keep(ref):
         def store(t, cells):
@@ -421,16 +448,18 @@
         loads[1 + c].wait()
         for y in range(ROWS):
             field_in[rows_of(c, y), :] = v_pad[c, y + 1].astype(bf16)
-        x_tiles(0, x_plain, (2 * c, 2 * c + 1))
+        x_tiles(0, x_plain, c)
     pl.semaphore_wait(barrier, PY - 1 + PZ - 1)
-    out_pz(0)
+    for c in range(3):
+        out_pz(0, c)
     halo_y_start(v_pad, 0)
-    for load in loads[4:]:
+    for load in loads[4:10]:
         load.wait()
     halo_z_start(v_pad, 0)
     z_stage(0)
     out_py(0)
     shifts(v_pad, v_shift, 0)
+    flatten_weight()
     modes = y_stage(0).astype(bf16)
     hat_v[...] = modes
     real, imag = curl(modes[:MODES].astype(f32), modes[MODES:].astype(f32))
@@ -438,7 +467,6 @@
     out_py(1)
     closure_rows(range(0, 4))
     z_back_stage(1)
-    out_pz(1)
 
     closure_rows(range(4, ROWS))
     for c in range(3):
@@ -454,19 +482,17 @@
         for c, cells in enumerate(cross(here, there)):
             field_in[rows_of(c, y), :] = cells.astype(bf16)
     x_stage(3, x_plain)
-    out_pz(3)
-    out_pz(2)
+    z_stage(2)
+    out_py(2)
     z_stage(3)
     out_py(3)
-    z_stage(2)
-    out_py(2)
+    again = y_stage(2)
     modes = y_stage(3).astype(bf16).astype(f32)
     drag = viscosity * square
     real = project(modes[:MODES]) - drag * hat_v[:MODES].astype(f32)
     imag = project(modes[MODES:]) - drag * hat_v[MODES:].astype(f32)
     rate_hat = jnp.concatenate([real, imag], axis=0).astype(bf16)
     twice = jnp.where(kx == 0.0, 1.0, 2.0) * (time_step * time_step)
-    again = y_stage(2)
     real = (again[:MODES] + twice * rate_hat[:MODES].astype(f32)).astype(bf16)
     imag = (again[MODES:] + twice * rate_hat[MODES:].astype(f32)).astype(bf16)
     hat_r[:MODES] = real
@@ -477,9 +503,7 @@
     y_back_stage(5, rate_hat)
     out_py(5)
     z_back_stage(4)
-    out_pz(4)
     z_back_stage(5)
-    out_pz(5)
 
     x_back_stage(4, x_plain, keep(push))
     for y in range(ROWS):
@@ -488,7 +512,6 @@
         for c, cells in enumerate(cross(there, here)):
             field_in[rows_of(c, y), :] = cells.astype(bf16)
     x_stage(6, x_twice)
-    out_pz(6)
 
     parts = [jnp.zeros((8, LANES), f32) for _ in range(4)]
 
@@ -508,10 +531,11 @@
     w_parts[246] = 0.5 * parts[3]
     for k in range(247, 256):
         w_parts[k] = jnp.zeros((8, LANES), f32)
+    weight_parts(0, 10)
     z_stage(6)
     out_py(6)
     halo_z_start(m_pad, 4)
-    weight_parts(0, 27)
+    weight_parts(10, 27)
     reduce_start()
     modes = y_stage(6).astype(bf16).astype(f32)
     real, imag = curl(modes[:MODES], modes[MODES:])
@@ -520,19 +544,23 @@
     y_back_stage(7, jnp.concatenate([real, imag], axis=0).astype(bf16))
     out_py(7)
     shifts(m_pad, m_shift, 4)
+    grad_rows(range(0, 2))
     reduce_next()
     z_back_stage(7)
-    out_pz(7, last_recv)
-    grad_rows(range(ROWS))
+    grad_rows(range(2, ROWS))
     for y in range(ROWS):
         here = [vort[rows_of(c, y), :] for c in range(3)]
         there = [push[rows_of(c, y), :] for c in range(3)]
         for c, cells in enumerate(cross(here, there)):
             closure[c, y] = closure[c, y] + m_pad[c, y + 1] + cells
-    base = pltpu.make_async_copy(closure, base_out, base_sem)
-    base.start()
     reduce_end()
-    arrived(last_recv, pz_rs.at[7])
+
+    def finish(t, cells):
+        for m in range(4):
+            y = (t % 2) * 4 + m
+            grad[t // 2, y] = closure[t // 2, y] + cells[m * DEPTH : (m + 1) * DEPTH]
+
+    x_back_stage(7, x_plain, finish)
 
     for n in range(8):
         arrived(pz_send.at[n, 0 : PZ - 1], pz_ss.at[n])
@@ -545,27 +573,6 @@
         arrived(halo_out.at[n // 4, 1], halo_ss.at[n + 3])
     arrived(r_pz.at[0 : PZ - 1], red_ss.at[0])
     arrived(r_py.at[0 : PY - 1], red_ss.at[1])
-    base.wait()
-
-
-def last_kernel(modes, base, table, sums, grad, grad_weight, grad_bias, loss):
-    block = modes[...].reshape(128, LANES)
-    cells = dot(block, table[...], ((0,), (0,)))
-    for m in range(4):
-        grad[0, m] = base[0, m] + cells[m * DEPTH : (m + 1) * DEPTH]
-
-    @pl.when(pl.program_id(0) == 0)
-    def _():
-        def one(t, _):
-            i, j, a = t // 27, (t // 9) % 3, (t // 3) % 3
-            for e in range(3):
-                grad_weight[i, j, a, t % 3, e] = sums[0, t * 3 + e]
-            return 0
-
-        lax.fori_loop(0, 81, one, 0)
-        for i in range(3):
-            grad_bias[i] = sums[0, 243 + i]
-        loss[0] = sums[0, 246]
 
 
 def on_device(velocity, target, closure_weight, closure_bias):
@@ -577,15 +584,16 @@
     pad = (3, ROWS + 2, DEPTH, NX)
     in_hbm = pl.BlockSpec(memory_space=pl.ANY)
     landing = (PZ, 6, 16, LANES)
-    base, modes, sums = pl.pallas_call(
+    grad, grad_weight, grad_bias, loss = pl.pallas_call(
         kernel,
         out_shape=(
             jax.ShapeDtypeStruct(shape, f32),
-            jax.ShapeDtypeStruct(landing, bf16),
-            jax.ShapeDtypeStruct((1, 256), f32),
+            jax.ShapeDtypeStruct(closure_weight.shape, f32),
+            jax.ShapeDtypeStruct((3,), f32),
+            jax.ShapeDtypeStruct((1,), f32),
         ),
-        in_specs=[in_hbm, in_hbm, in_smem, in_smem] + [in_hbm] * 6,
-        out_specs=(in_hbm, in_hbm, in_vmem),
+        in_specs=[in_hbm, in_hbm, in_hbm, in_smem] + [in_hbm] * 6,
+        out_specs=(in_vmem, in_vmem, in_smem, in_smem),
         scratch_shapes=[pltpu.VMEM(t.shape, bf16) for t in given]
         + [
             pltpu.VMEM(shape, f32),
@@ -613,33 +621,15 @@
             pltpu.VMEM((PY, 1, 256), f32),
             pltpu.VMEM((256, LANES), bf16),
             pltpu.VMEM((256, LANES), bf16),
-            dma((8,)), dma((8,)), dma((8,)), dma((8,)), dma((8,)), dma((8,)), dma((2,)), dma((2,)),
-            dma((10,)), dma,
+            dma((8,)), dma((8, 3)), dma((8,)), dma((8,)), dma((8,)), dma((8,)), dma((2,)), dma((2,)),
+            dma((11,)), pltpu.SMEM(closure_weight.shape, f32),
+            pltpu.SMEM((243,), f32),
         ],
         compiler_params=pltpu.CompilerParams(
             collective_id=0, has_side_effects=True, vmem_limit_bytes=56 << 20
         ),
         name="euler",
     )(velocity, target, closure_weight, closure_bias, *given)
-    half = pl.BlockSpec((1, 4, DEPTH, NX), lambda t: (t // 2, t % 2, 0, 0))
-    grad, grad_weight, grad_bias, loss = pl.pallas_call(
-        last_kernel,
-        grid=(6,),
-        out_shape=(
-            jax.ShapeDtypeStruct(shape, f32),
-            jax.ShapeDtypeStruct(closure_weight.shape, f32),
-            jax.ShapeDtypeStruct((3,), f32),
-            jax.ShapeDtypeStruct((1,), f32),
-        ),
-        in_specs=[
-            pl.BlockSpec((PZ, 1, 16, LANES), lambda t: (0, t, 0, 0)),
-            half,
-            pl.BlockSpec((128, NX), lambda t: (0, 0)),
-            in_smem,
-        ],
-        out_specs=(half, in_smem, in_smem, in_smem),
-        name="last",
-    )(modes, base, given[0], sums)
     return grad, grad_weight, grad_bias, loss.reshape(())
 
 

time: 109 us -> 96.3 us (0.88)
  Pallas kernels: 108 us -> 90.4 us
  local copies, waits for them, and re-layouts: 0 us -> 3.28 us
  between operations: 0.64 us -> 2.38 us
    pallas_call x1, Pallas kernels: 99.6 us -> 90.4 us  [on_device(): pl.pallas_call(kernel, out_shape=(jax.ShapeDtypeStruct(shape, f32), jax.S...]
    pallas_call x1 -> x0, Pallas kernels: 8.54 us -> none  [on_device(): pl.pallas_call(last_kernel, grid=(6,), out_shape=(jax.ShapeDtypeStruct(sh...]
    unnamed x0 -> x7, local copies, waits for them, and re-layouts: none -> 3.28 us
where the time goes in v3:
time: 96.3 us; the launch traced here: 96.1 us
  Pallas kernels  90.4 us (94%)
  local copies, waits for them, and re-layouts  3.28 us (3%)
  between operations  2.38 us (2%)
    pallas_call x1, Pallas kernels, on_device(): pl.pallas_call(kernel, out_shape=(jax.ShapeDtypeStruct(shape, f32), jax.S...  90.4 us
    unnamed x7, local copies, waits for them, and re-layouts  3.28 us

profile of v3, /device:TPU:1, one launch (start us, length us, event | category | flops | bytes accessed | tf_op | source)
XLA Modules:
  0.0 96.1 jit_solution(3706222487677442029)
XLA Ops:
  0.6 90.4 %euler.1 = (f32[3,8,32,256]{3,2,1,0:T(8,128)}, f32[3,3,3,3,3]{4,3,2,1,0:T(4,128)}, f32[3]{0:T(128)}, f32[1]{0:T(128)}) custom-call(f32[3,8,32,256]{3,2,1,0:T(8,128)} %vel_in.1, f32[3,8,32,256]{3,2,1,0:T(8,128)} %target_in.1, f32[3,3,3,3,3]{4,3,2,1,0:T(4,128)} %weight_in.1, f32[3]{0:T(128)} %bias.1, bf16[128,256]{1,0:T(8,128)(2,1)} %constant.12.clone.refs_0_, ...), custom_call_target="tpu_custom_call" | custom-call | tf_op jit(solution)/shard_map/euler/pallas_call | solution.py:587
  91.1 0.0 copy-start
  91.1 2.1 %copy.18 = f32[3,8,32,256]{3,2,1,0:T(8,128)} copy(f32[3,8,32,256]{3,2,1,0:T(8,128)} %get-tuple-element.16) | data formatting | bytes 1572864
  93.2 0.0 copy-done
  93.2 0.0 copy-start.1
  93.2 0.6 copy.19
  93.8 0.0 copy-done.1
  93.9 0.5 copy.20
Async XLA Ops:
  91.1 2.1 %copy-start = (f32[3,3,3,3,3]{4,3,2,1,0:T(4,128)S(1)}, f32[3,3,3,3,3]{4,3,2,1,0:T(4,128)}, u32[]{:S(2)}) copy-start(f32[3,3,3,3,3]{4,3,2,1,0:T(4,128)} %get-tuple-element.17) | copy-start | bytes 2920
  93.2 0.7 copy-start.1

commit v4 on v3

--- a/solution.py
+++ b/solution.py
@@ -327,19 +327,14 @@
         part = part + next_one(part) + next_two(part)
         return cells - along * (part / jnp.maximum(square, 1.0))
 
-    def out_pz(n, c):
-        tiles = pl.ds(2 * c, 2)
-        send_pz(
-            lambda to: pz_send.at[n, to, tiles], pz_recv.at[n, pz, tiles], pz_ss.at[n],
-            pz_rs.at[n, c],
-        )
+    def out_pz(n):
+        send_pz(lambda to: pz_send.at[n, to], pz_recv.at[n, pz], pz_ss.at[n], pz_rs.at[n])
 
     def out_py(n):
         send_py(lambda to: py_send.at[n, to], py_recv.at[n], py_ss.at[n], py_rs.at[n])
 
-    def in_pz(n, c):
-        here = pz_recv.at[n, :, pl.ds(2 * c, 2)]
-        arrived(here, pz_rs.at[n, c])
+    def in_pz(n):
+        arrived(pz_recv.at[n], pz_rs.at[n])
 
     def in_py(n):
         arrived(py_recv.at[n], py_rs.at[n])
@@ -347,7 +342,7 @@
     def x_stage(n, table):
         for c in range(3):
             x_tiles(n, table, c)
-            out_pz(n, c)
+        out_pz(n)
 
     def x_tiles(n, table, c):
         for t in (2 * c, 2 * c + 1):
@@ -357,8 +352,8 @@
                 pz_send[n, p, t] = out[p * 16 : (p + 1) * 16]
 
     def z_stage(n):
+        in_pz(n)
         for c in range(3):
-            in_pz(n, c)
             for yh in range(2):
                 for h in range(2):
                     tiles = [pz_recv[n, 4 * h + g, 2 * c + yh].astype(f32) for g in range(4)]
@@ -417,11 +412,11 @@
                     ]
                     for g, tile in enumerate(swap_groups(tiles, lane16)):
                         pz_send[n, half * 4 + g, c * 2 + h] = tile.astype(bf16)
-            out_pz(n, c)
+        out_pz(n)
 
     def x_back_stage(n, table, out):
+        in_pz(n)
         for c in range(3):
-            in_pz(n, c)
             for t in (2 * c, 2 * c + 1):
                 block = pz_recv[n, :, t].reshape(128, LANES)
                 out(t, dot(block, table[...], ((0,), (0,))))
@@ -450,8 +445,7 @@
             field_in[rows_of(c, y), :] = v_pad[c, y + 1].astype(bf16)
         x_tiles(0, x_plain, c)
     pl.semaphore_wait(barrier, PY - 1 + PZ - 1)
-    for c in range(3):
-        out_pz(0, c)
+    out_pz(0)
     halo_y_start(v_pad, 0)
     for load in loads[4:10]:
         load.wait()
@@ -465,10 +459,9 @@
     real, imag = curl(modes[:MODES].astype(f32), modes[MODES:].astype(f32))
     y_back_stage(1, jnp.concatenate([real, imag], axis=0).astype(bf16))
     out_py(1)
-    closure_rows(range(0, 4))
+    closure_rows(range(ROWS))
     z_back_stage(1)
 
-    closure_rows(range(4, ROWS))
     for c in range(3):
         for y in range(ROWS):
             cells = v_pad[c, y + 1] + closure[c, y] - target[c, y]
@@ -531,11 +524,11 @@
     w_parts[246] = 0.5 * parts[3]
     for k in range(247, 256):
         w_parts[k] = jnp.zeros((8, LANES), f32)
-    weight_parts(0, 10)
+    weight_parts(0, 6)
     z_stage(6)
     out_py(6)
     halo_z_start(m_pad, 4)
-    weight_parts(10, 27)
+    weight_parts(6, 27)
     reduce_start()
     modes = y_stage(6).astype(bf16).astype(f32)
     real, imag = curl(modes[:MODES], modes[MODES:])
@@ -544,10 +537,10 @@
     y_back_stage(7, jnp.concatenate([real, imag], axis=0).astype(bf16))
     out_py(7)
     shifts(m_pad, m_shift, 4)
-    grad_rows(range(0, 2))
+    grad_rows(range(0, 3))
     reduce_next()
     z_back_stage(7)
-    grad_rows(range(2, ROWS))
+    grad_rows(range(3, ROWS))
     for y in range(ROWS):
         here = [vort[rows_of(c, y), :] for c in range(3)]
         there = [push[rows_of(c, y), :] for c in range(3)]
@@ -621,7 +614,7 @@
             pltpu.VMEM((PY, 1, 256), f32),
             pltpu.VMEM((256, LANES), bf16),
             pltpu.VMEM((256, LANES), bf16),
-            dma((8,)), dma((8, 3)), dma((8,)), dma((8,)), dma((8,)), dma((8,)), dma((2,)), dma((2,)),
+            dma((8,)), dma((8,)), dma((8,)), dma((8,)), dma((8,)), dma((8,)), dma((2,)), dma((2,)),
             dma((11,)), pltpu.SMEM(closure_weight.shape, f32),
             pltpu.SMEM((243,), f32),
         ],

time: 96.3 us -> 94 us (0.976)
  Pallas kernels: 90.4 us -> 88.1 us
    pallas_call x1, Pallas kernels: 90.4 us -> 88.1 us  [on_device(): pl.pallas_call(kernel, out_shape=(jax.ShapeDtypeStruct(shape, f32), jax.S...]
where the time goes in v4:
time: 94 us; the launch traced here: 93.8 us
  Pallas kernels  88.1 us (94%)
  local copies, waits for them, and re-layouts  3.28 us (3%)
  between operations  2.38 us (3%)
    pallas_call x1, Pallas kernels, on_device(): pl.pallas_call(kernel, out_shape=(jax.ShapeDtypeStruct(shape, f32), jax.S...  88.1 us
    unnamed x7, local copies, waits for them, and re-layouts  3.28 us

profile of v4, /device:TPU:1, one launch (start us, length us, event | category | flops | bytes accessed | tf_op | source)
XLA Modules:
  0.0 93.8 jit_solution(330349484679824728)
XLA Ops:
  0.6 88.1 %euler.1 = (f32[3,8,32,256]{3,2,1,0:T(8,128)}, f32[3,3,3,3,3]{4,3,2,1,0:T(4,128)}, f32[3]{0:T(128)}, f32[1]{0:T(128)}) custom-call(f32[3,8,32,256]{3,2,1,0:T(8,128)} %vel_in.1, f32[3,8,32,256]{3,2,1,0:T(8,128)} %target_in.1, f32[3,3,3,3,3]{4,3,2,1,0:T(4,128)} %weight_in.1, f32[3]{0:T(128)} %bias.1, bf16[128,256]{1,0:T(8,128)(2,1)} %constant.12.clone.refs_0_, ...), custom_call_target="tpu_custom_call" | custom-call | tf_op jit(solution)/shard_map/euler/pallas_call | solution.py:580
  88.8 0.0 copy-start
  88.8 2.1 %copy.18 = f32[3,8,32,256]{3,2,1,0:T(8,128)} copy(f32[3,8,32,256]{3,2,1,0:T(8,128)} %get-tuple-element.16) | data formatting | bytes 1572864
  90.9 0.0 copy-done
  90.9 0.0 copy-start.1
  90.9 0.6 copy.19
  91.5 0.0 copy-done.1
  91.6 0.5 copy.20
Async XLA Ops:
  88.8 2.1 %copy-start = (f32[3,3,3,3,3]{4,3,2,1,0:T(4,128)S(1)}, f32[3,3,3,3,3]{4,3,2,1,0:T(4,128)}, u32[]{:S(2)}) copy-start(f32[3,3,3,3,3]{4,3,2,1,0:T(4,128)} %get-tuple-element.17) | copy-start | bytes 2920
  90.9 0.7 copy-start.1

commit v5 on v4

--- a/solution.py
+++ b/solution.py
@@ -368,7 +368,7 @@
                 stage[c, 1, pl.ds(y, 8, stride=8), :] = r0[:, 128:] + r1[:, :128]
         blocks = [
             swap_groups(
-                [stage[0, q], stage[1, q], stage[2, q], jnp.zeros((64, LANES), f32)], lane64
+                [stage[c, q, 0:64] for c in range(3)] + [jnp.zeros((64, LANES), f32)], lane64
             )
             for q in range(2)
         ]
@@ -596,8 +596,8 @@
             pltpu.VMEM((8, PY, 16, LANES), bf16),
             pltpu.VMEM((768, NX), bf16),
             pltpu.VMEM((384, 256), bf16),
-            pltpu.VMEM((3, 2, 64, LANES), f32),
-            pltpu.VMEM((3, 2, 128, LANES), f32),
+            pltpu.VMEM((3, 2, 72, LANES), f32),
+            pltpu.VMEM((3, 2, 144, LANES), f32),
             pltpu.VMEM((768, NX), f32),
             pltpu.VMEM((768, NX), f32),
             pltpu.VMEM(pad, f32),

time: 94 us -> 94 us (level)
  no operation moved by 1% of the time
where the time goes in v5:
time: 94 us; the launch traced here: 93.9 us
  Pallas kernels  88.2 us (94%)
  local copies, waits for them, and re-layouts  3.28 us (3%)
  between operations  2.38 us (3%)
    pallas_call x1, Pallas kernels, on_device(): pl.pallas_call(kernel, out_shape=(jax.ShapeDtypeStruct(shape, f32), jax.S...  88.2 us
    unnamed x7, local copies, waits for them, and re-layouts  3.28 us

profile of v5, /device:TPU:1, one launch (start us, length us, event | category | flops | bytes accessed | tf_op | source)
XLA Modules:
  0.0 93.9 jit_solution(3981213248937128241)
XLA Ops:
  0.6 88.2 %euler.1 = (f32[3,8,32,256]{3,2,1,0:T(8,128)}, f32[3,3,3,3,3]{4,3,2,1,0:T(4,128)}, f32[3]{0:T(128)}, f32[1]{0:T(128)}) custom-call(f32[3,8,32,256]{3,2,1,0:T(8,128)} %vel_in.1, f32[3,8,32,256]{3,2,1,0:T(8,128)} %target_in.1, f32[3,3,3,3,3]{4,3,2,1,0:T(4,128)} %weight_in.1, f32[3]{0:T(128)} %bias.1, bf16[128,256]{1,0:T(8,128)(2,1)} %constant.12.clone.refs_0_, ...), custom_call_target="tpu_custom_call" | custom-call | tf_op jit(solution)/shard_map/euler/pallas_call | solution.py:580
  88.8 0.0 copy-start
  88.8 2.1 %copy.18 = f32[3,8,32,256]{3,2,1,0:T(8,128)} copy(f32[3,8,32,256]{3,2,1,0:T(8,128)} %get-tuple-element.16) | data formatting | bytes 1572864
  90.9 0.0 copy-done
  91.0 0.0 copy-start.1
  91.0 0.6 copy.19
  91.6 0.0 copy-done.1
  91.6 0.5 copy.20
Async XLA Ops:
  88.8 2.1 %copy-start = (f32[3,3,3,3,3]{4,3,2,1,0:T(4,128)S(1)}, f32[3,3,3,3,3]{4,3,2,1,0:T(4,128)}, u32[]{:S(2)}) copy-start(f32[3,3,3,3,3]{4,3,2,1,0:T(4,128)} %get-tuple-element.17) | copy-start | bytes 2920
  91.0 0.7 copy-start.1

commit v6 on v4

--- a/solution.py
+++ b/solution.py
@@ -518,7 +518,6 @@
             parts[3] = parts[3] + fold(cells * cells)
 
     x_back_stage(5, x_twice, misfit)
-    halo_y_start(m_pad, 4)
     for c in range(3):
         w_parts[243 + c] = parts[c]
     w_parts[246] = 0.5 * parts[3]
@@ -527,8 +526,9 @@
     weight_parts(0, 6)
     z_stage(6)
     out_py(6)
+    halo_y_start(m_pad, 4)
+    weight_parts(6, 27)
     halo_z_start(m_pad, 4)
-    weight_parts(6, 27)
     reduce_start()
     modes = y_stage(6).astype(bf16).astype(f32)
     real, imag = curl(modes[:MODES], modes[MODES:])

time: 94 us -> 94.9 us (level)
  no operation moved by 1% of the time
where the time goes in v6:
time: 94.9 us; the launch traced here: 94.7 us
  Pallas kernels  89 us (94%)
  local copies, waits for them, and re-layouts  3.28 us (3%)
  between operations  2.38 us (3%)
    pallas_call x1, Pallas kernels, on_device(): pl.pallas_call(kernel, out_shape=(jax.ShapeDtypeStruct(shape, f32), jax.S...  89 us
    unnamed x7, local copies, waits for them, and re-layouts  3.28 us

profile of v6, /device:TPU:1, one launch (start us, length us, event | category | flops | bytes accessed | tf_op | source)
XLA Modules:
  0.0 94.7 jit_solution(4772881441959366315)
XLA Ops:
  0.6 89.0 %euler.1 = (f32[3,8,32,256]{3,2,1,0:T(8,128)}, f32[3,3,3,3,3]{4,3,2,1,0:T(4,128)}, f32[3]{0:T(128)}, f32[1]{0:T(128)}) custom-call(f32[3,8,32,256]{3,2,1,0:T(8,128)} %vel_in.1, f32[3,8,32,256]{3,2,1,0:T(8,128)} %target_in.1, f32[3,3,3,3,3]{4,3,2,1,0:T(4,128)} %weight_in.1, f32[3]{0:T(128)} %bias.1, bf16[128,256]{1,0:T(8,128)(2,1)} %constant.12.clone.refs_0_, ...), custom_call_target="tpu_custom_call" | custom-call | tf_op jit(solution)/shard_map/euler/pallas_call | solution.py:580
  89.7 0.0 copy-start
  89.7 2.1 %copy.18 = f32[3,8,32,256]{3,2,1,0:T(8,128)} copy(f32[3,8,32,256]{3,2,1,0:T(8,128)} %get-tuple-element.16) | data formatting | bytes 1572864
  91.8 0.0 copy-done
  91.8 0.0 copy-start.1
  91.8 0.6 copy.19
  92.4 0.0 copy-done.1
  92.4 0.5 copy.20
Async XLA Ops:
  89.7 2.1 %copy-start = (f32[3,3,3,3,3]{4,3,2,1,0:T(4,128)S(1)}, f32[3,3,3,3,3]{4,3,2,1,0:T(4,128)}, u32[]{:S(2)}) copy-start(f32[3,3,3,3,3]{4,3,2,1,0:T(4,128)} %get-tuple-element.17) | copy-start | bytes 2920
  91.8 0.7 copy-start.1

commit v7 on v4

--- a/solution.py
+++ b/solution.py
@@ -140,16 +140,22 @@
             device_id_type=MESH,
         )
 
+    x, z, core = py // 16, lax.rem(py, 16) // 2, lax.rem(py, 2)
+    far_py = [
+        lax.rem(x + dx, 2) * 16 + lax.rem(z + dz, 8) * 2 + lax.rem(core + dc, 2)
+        for dx, dz, dc in FAR_PY
+    ]
+    far_pz = [
+        lax.rem(pz // 4 + dx, 2) * 4 + lax.rem(lax.rem(pz, 4) + dy, 4) for dx, dy in FAR_PZ
+    ]
+
     def send_pz(send_of, landing, ss, rs):
-        for dx, dy in FAR_PZ:
-            to = lax.rem(pz // 4 + dx, 2) * 4 + lax.rem(lax.rem(pz, 4) + dy, 4)
+        for to in far_pz:
             remote(send_of(to), landing, ss, rs, (py, to)).start()
         pltpu.make_async_copy(send_of(pz), landing, rs).start()
 
     def send_py(send_of, recv, ss, rs):
-        x, z, core = py // 16, lax.rem(py, 16) // 2, lax.rem(py, 2)
-        for dx, dz, dc in FAR_PY:
-            to = lax.rem(x + dx, 2) * 16 + lax.rem(z + dz, 8) * 2 + lax.rem(core + dc, 2)
+        for to in far_py:
             remote(send_of(to), recv.at[py], ss, rs, (to, pz)).start()
         pltpu.make_async_copy(send_of(py), recv.at[py], rs).start()
 
@@ -321,11 +327,13 @@
     def curl(real, imag):
         return -turned(imag), turned(real)
 
+    along = pick(kx, ky, kz)
+    share = along / jnp.maximum(square, 1.0)
+
     def project(cells):
-        along = pick(kx, ky, kz)
         part = along * cells
         part = part + next_one(part) + next_two(part)
-        return cells - along * (part / jnp.maximum(square, 1.0))
+        return cells - share * part
 
     def out_pz(n):
         send_pz(lambda to: pz_send.at[n, to], pz_recv.at[n, pz], pz_ss.at[n], pz_rs.at[n])
@@ -360,10 +368,11 @@
                     for m, tile in enumerate(swap_groups(tiles, lane16)):
                         at = c * 128 + (yh * 4 + m) * 16
                         z_in[at : at + 16, h * 128 : (h + 1) * 128] = tile.astype(bf16)
-            both = dot(z_in[c * 128 : (c + 1) * 128, :], z_out[...], ((1,), (0,)))
+        whole = dot(z_in[...], z_out[...], ((1,), (0,)))
+        for c in range(3):
             for y in range(ROWS):
-                r0 = both[y * 16 : y * 16 + 8]
-                r1 = both[y * 16 + 8 : y * 16 + 16]
+                r0 = whole[c * 128 + y * 16 : c * 128 + y * 16 + 8]
+                r1 = whole[c * 128 + y * 16 + 8 : c * 128 + y * 16 + 16]
                 stage[c, 0, pl.ds(y, 8, stride=8), :] = r0[:, :128] - r1[:, 128:]
                 stage[c, 1, pl.ds(y, 8, stride=8), :] = r0[:, 128:] + r1[:, :128]
         blocks = [
@@ -394,8 +403,9 @@
             for c, tile in enumerate(swap_groups(tiles, lane16)[:3]):
                 at = c * 128 + k * 16
                 z_in[at : at + 16, 0:128] = tile.astype(bf16)
+        whole = dot(z_in[:, 0:128], z_back[...], ((1,), (0,)))
         for c in range(3):
-            both = dot(z_in[c * 128 : (c + 1) * 128, 0:128], z_back[...], ((1,), (0,)))
+            both = whole[c * 128 : (c + 1) * 128]
             for k in range(KL):
                 r0 = both[k * 16 : k * 16 + 8]
                 r1 = both[k * 16 + 8 : k * 16 + 16]

time: 94 us -> 93.5 us (level)
  no operation moved by 1% of the time
where the time goes in v7:
time: 93.5 us; the launch traced here: 93.4 us
  Pallas kernels  87.7 us (94%)
  local copies, waits for them, and re-layouts  3.28 us (4%)
  between operations  2.38 us (3%)
    pallas_call x1, Pallas kernels, on_device(): pl.pallas_call(kernel, out_shape=(jax.ShapeDtypeStruct(shape, f32), jax.S...  87.7 us
    unnamed x7, local copies, waits for them, and re-layouts  3.28 us

profile of v7, /device:TPU:1, one launch (start us, length us, event | category | flops | bytes accessed | tf_op | source)
XLA Modules:
  0.0 93.4 jit_solution(16121263337109015442)
XLA Ops:
  0.6 87.7 %euler.1 = (f32[3,8,32,256]{3,2,1,0:T(8,128)}, f32[3,3,3,3,3]{4,3,2,1,0:T(4,128)}, f32[3]{0:T(128)}, f32[1]{0:T(128)}) custom-call(f32[3,8,32,256]{3,2,1,0:T(8,128)} %vel_in.1, f32[3,8,32,256]{3,2,1,0:T(8,128)} %target_in.1, f32[3,3,3,3,3]{4,3,2,1,0:T(4,128)} %weight_in.1, f32[3]{0:T(128)} %bias.1, bf16[128,256]{1,0:T(8,128)(2,1)} %constant.12.clone.refs_0_, ...), custom_call_target="tpu_custom_call" | custom-call | tf_op jit(solution)/shard_map/euler/pallas_call | solution.py:590
  88.4 0.0 copy-start
  88.4 2.1 %copy.18 = f32[3,8,32,256]{3,2,1,0:T(8,128)} copy(f32[3,8,32,256]{3,2,1,0:T(8,128)} %get-tuple-element.16) | data formatting | bytes 1572864
  90.5 0.0 copy-done
  90.5 0.0 copy-start.1
  90.5 0.6 copy.19
  91.1 0.0 copy-done.1
  91.1 0.5 copy.20
Async XLA Ops:
  88.4 2.1 %copy-start = (f32[3,3,3,3,3]{4,3,2,1,0:T(4,128)S(1)}, f32[3,3,3,3,3]{4,3,2,1,0:T(4,128)}, u32[]{:S(2)}) copy-start(f32[3,3,3,3,3]{4,3,2,1,0:T(4,128)} %get-tuple-element.17) | copy-start | bytes 2920
  90.5 0.7 copy-start.1
